TPU v7x, 32 devices: a whole 2x2x4 slice. The times are simulated.
32 devices in a mesh: row: 4 (over y, core), col: 8 (over z, x).
Axes of the slice: x: 2, y: 2, z: 4, core: 2. Of those that a mesh axis runs over, the one named last changes fastest.
Arguments:
- points: float32 [4, 4, 256, 128], P(None, 'row'), may hold values from -1 to 1
- rhs: float32 [4, 4, 256, 256], P(None, 'row', None, 'col'), may hold values from -6 to 6
Outputs:
- factored: float32 [4, 4, 256, 2, 8, 256], P(None, 'row', None, None, 'col')
- solved: float32 [4, 4, 256, 256], P(None, 'row', None, 'col')
All inputs are finite; a program needn't handle non-finite values.
Results may differ from a plain program's by a relative error of at most 0.0003.
Values sent between devices are 32-bit elements; how exact they have to be, the bound alone decides.
A program may use at most 64 MiB of HBM per device.

v0:
```python
import functools

import jax
import jax.numpy as jnp
from jax import lax
from jax.experimental import pallas as pl
from jax.experimental.pallas import tpu as pltpu
from jax.sharding import PartitionSpec as P

PANELS = 2
SCALE = 3.0
NUGGET = 1.0
HIGHEST = lax.Precision.HIGHEST
MESH = pl.DeviceIdType.MESH
F32 = jnp.float32
BF16 = jnp.bfloat16
NB = 128


def fetch_kernel(rows_n, cols_n, tile_cols, pts, prhs, piv, colp, rpiv, send, recv, local):
    row_id = lax.axis_index("row")
    col_id = lax.axis_index("col")
    stride = cols_n // rows_n

    barrier = pltpu.get_barrier_semaphore()
    for step in range(1, rows_n):
        other = lax.rem(row_id + step, rows_n)
        pl.semaphore_signal(barrier, inc=1, device_id={"row": other}, device_id_type=MESH)
    pl.semaphore_wait(barrier, rows_n - 1)

    jobs = []
    for k in range(PANELS):
        jobs.append((k % rows_n, pts.at[k // rows_n], piv.at[k]))
        jobs.append((k % rows_n, prhs.at[k // rows_n], rpiv.at[k]))
    for c2 in range(tile_cols):
        slot = c2 * stride + col_id // rows_n
        jobs.append((lax.rem(col_id, rows_n), pts.at[slot], colp.at[c2]))

    chips = rows_n // 2
    chip, core = row_id // 2, lax.rem(row_id, 2)
    sibling = row_id + 1 - 2 * core

    def half_of(ref, half):
        height = ref.shape[0] // 2
        return ref.at[pl.ds(pl.multiple_of(half * height, height), height)]

    def remote(number, half, dest, slot, relay=False):
        _, src, dst = jobs[number]
        return pltpu.make_async_remote_copy(
            src_ref=half_of(dst if relay else src, half),
            dst_ref=half_of(dst, half),
            send_sem=send.at[number, slot],
            recv_sem=recv.at[number, half],
            device_id={"row": dest},
            device_id_type=MESH,
        )

    def sends(number):
        out = []
        for step in range(1, chips):
            for half in range(2):
                dest = 2 * lax.rem(chip + step, chips) + half
                out.append(remote(number, half, dest, 2 * step + half))
        return out + [remote(number, half, sibling, half) for half in range(2)]

    for number, (owner, src, dst) in enumerate(jobs):

        @pl.when(row_id == owner)
        def _(number=number, src=src, dst=dst):
            for copy in sends(number):
                copy.start()
            pltpu.make_async_copy(src, dst, local.at[number]).start()

    for number, (owner, src, dst) in enumerate(jobs):

        @pl.when(chip != owner // 2)
        def _(number=number):
            relay = remote(number, core, sibling, 0, relay=True)
            relay.wait_recv()
            relay.start()

    for number, (owner, src, dst) in enumerate(jobs):

        @pl.when(row_id == owner)
        def _(number=number, src=src, dst=dst):
            for copy in sends(number):
                copy.wait_send()
            pltpu.make_async_copy(src, dst, local.at[number]).wait()

        @pl.when(sibling == owner)
        def _(number=number):
            for half in range(2):
                remote(number, half, sibling, half).wait_recv()

        @pl.when(chip != owner // 2)
        def _(number=number):
            remote(number, core, sibling, 0, relay=True).wait_send()
            remote(number, 1 - core, sibling, 0, relay=True).wait_recv()


def split(x):
    hi = x.astype(BF16)
    return hi, (x - hi.astype(F32)).astype(BF16)


def nt(a, b):
    return lax.dot_general(a, b, (((1,), (1,)), ((), ())), preferred_element_type=F32)


def nt3(a, b):
    return nt(a[0], b[0]) + (nt(a[0], b[1]) + nt(a[1], b[0]))


def squared_exp(a, b, b_sq):
    a_sq = jnp.sum(a * a, axis=1, keepdims=True)
    inner = nt3(split(a), split(b))
    return jnp.exp((-SCALE / a.shape[1]) * (a_sq + b_sq - 2.0 * inner))


def row_squares(b):
    ones = jnp.ones((8, b.shape[1]), F32)
    return lax.dot_general(
        ones, b * b, (((1,), (1,)), ((), ())), precision=HIGHEST, preferred_element_type=F32
    )[:1]


def spread(column):
    return jnp.broadcast_to(column, (column.shape[0], 2 * NB))


def base_inverse(block, base):
    eye = (
        lax.broadcasted_iota(jnp.int32, (NB, NB), 0) == lax.broadcasted_iota(jnp.int32, (NB, NB), 1)
    ).astype(F32)
    wide = jnp.concatenate([block, eye], axis=1)
    v = [wide[8 * q : 8 * q + 8] for q in range(NB // 8)]
    for j in range(0, NB, 4):
        q0, s = divmod(j, 8)
        cols = [[spread(v[q][:, j + n : j + n + 1]) for n in range(4)] for q in range(q0, NB // 8)]
        rows = [v[q0][s + n : s + n + 1] for n in range(4)]
        at = [[cols[0][n][s + m : s + m + 1] for n in range(4)] for m in range(4)]

        def pair(r0, r1, a, b, b1, c, where):
            det = a * c - b * b1
            inv_det = 1.0 / det
            e1 = a * r1 - b1 * r0
            rs = lax.rsqrt(a)
            base[where : where + 1, :] = r0 * rs
            base[where + 1 : where + 2, :] = e1 * (lax.rsqrt(det) * rs)
            return a, b, b1, c, inv_det, (c * r0 - b * r1) * inv_det, e1 * inv_det

        a, b, b1, c, inv_det, s0, s1 = pair(
            rows[0], rows[1], at[0][0], at[0][1], at[1][0], at[1][1], j
        )
        u0 = [(c * at[0][n] - b * at[1][n]) * inv_det for n in (2, 3)]
        u1 = [(a * at[1][n] - b1 * at[0][n]) * inv_det for n in (2, 3)]
        r2, r3 = (rows[m] - at[m][0] * s0 - at[m][1] * s1 for m in (2, 3))
        p = [[at[m][n + 2] - at[m][0] * u0[n] - at[m][1] * u1[n] for n in (0, 1)] for m in (2, 3)]
        s2, s3 = pair(r2, r3, p[0][0], p[0][1], p[1][0], p[1][1], j + 2)[5:]
        for q in range(q0 if s == 0 else q0 + 1, NB // 8):
            k0, k1, k2, k3 = cols[q - q0]
            k2 = k2 - k0 * u0[0] - k1 * u1[0]
            k3 = k3 - k0 * u0[1] - k1 * u1[1]
            v[q] = v[q] - k0 * s0 - k1 * s1 - k2 * s2 - k3 * s3
    return base[:, NB:]


def inverse_factor(w, h, base):
    size = h.shape[0]
    for j0 in range(0, size, NB):
        j1 = j0 + NB
        inv = base_inverse(w[j0:j1, j0:j1], base)
        rows = jnp.dot(inv, w[j0:j1, :], precision=HIGHEST, preferred_element_type=F32)
        h[j0:j1, :] = rows[:, size:]
        if j1 < size:
            panel = lax.dot_general(
                w[j1:, j0:j1], inv, (((1,), (1,)), ((), ())), precision=HIGHEST, preferred_element_type=F32
            )
            w[j1:, :] = w[j1:, :] - jnp.dot(
                panel, rows, precision=HIGHEST, preferred_element_type=F32
            )


def main_kernel(
    rows_n, cols_n, hpts, hpiv, hcolp, hrhs, hrpiv, out, solved,
    pts, piv, colp, rhs, rpiv, sems, base, w, h0, h1, l10, lf, lh, ll, yh, yl,
):
    copies = [
        pltpu.make_async_copy(src, dst, sems.at[n])
        for n, (src, dst) in enumerate(
            ((hpiv, piv), (hrpiv, rpiv), (hcolp, colp), (hpts, pts), (hrhs, rhs))
        )
    ]
    for copy in copies:
        copy.start()
    copies[0].wait()
    row_id = lax.axis_index("row")
    col_id = lax.axis_index("col")
    tile_rows, size, _ = pts.shape
    tile_cols = colp.shape[0]
    row_in = lax.broadcasted_iota(jnp.int32, (size, size), 0)
    col_in = lax.broadcasted_iota(jnp.int32, (size, size), 1)
    eye = (row_in == col_in).astype(F32)
    lower = row_in >= col_in
    x0, x1 = piv[0], piv[1]
    sq0, sq1 = row_squares(x0), row_squares(x1)

    w[:, :size] = squared_exp(x0, x0, sq0) + NUGGET * eye
    w[:, size:] = eye
    inverse_factor(w, h0, base)
    h0s = split(h0[...])
    l10[...] = nt3(split(squared_exp(x1, x0, sq0)), h0s)
    l10s = split(l10[...])
    w[:, :size] = squared_exp(x1, x1, sq1) + NUGGET * eye - nt3(l10s, l10s)
    w[:, size:] = eye
    inverse_factor(w, h1, base)
    h1s = split(h1[...])

    for copy in copies[1:]:
        copy.wait()
    y0 = nt3(split(rpiv[0]), h0s)
    y1 = nt3(split(rpiv[1] - nt3(split(y0), l10s)), h1s)
    yh[:, :size], yl[:, :size] = split(y0)
    yh[:, size:], yl[:, size:] = split(y1)

    def panels_of(x, tile):
        k0 = squared_exp(x, x0, sq0) + jnp.where(tile == 0, NUGGET, 0.0) * eye
        l0 = nt3(split(k0), h0s)
        l0 = jnp.where((tile != 0) | lower, l0, 0.0)
        k1 = squared_exp(x, x1, sq1) + jnp.where(tile == 1, NUGGET, 0.0) * eye
        l1 = nt3(split(k1 - nt3(split(l0), l10s)), h1s)
        l1 = jnp.where((tile > 1) | (lower & (tile == 1)), l1, 0.0)
        return l0, l1

    @pl.loop(0, tile_cols)
    def _(c2):
        l0, l1 = panels_of(colp[c2], c2 * cols_n + col_id)
        lh[c2, :, :size], ll[c2, :, :size] = split(l0)
        lh[c2, :, size:], ll[c2, :, size:] = split(l1)

    @pl.loop(0, tile_rows)
    def _(a):
        tile = a * rows_n + row_id
        x = pts[a]
        l0, l1 = panels_of(x, tile)
        lf[:, :size] = l0
        lf[:, size:] = l1
        ls = split(lf[...])
        rest = rhs[a] - nt3((yh[...], yl[...]), ls)
        solved[a] = jnp.where(tile == 0, y0, jnp.where(tile == 1, y1, rest))
        for c2 in range(tile_cols):
            tile_c = c2 * cols_n + col_id
            xc = colp[c2]
            k = squared_exp(x, xc, row_squares(xc)) + jnp.where(tile == tile_c, NUGGET, 0.0) * eye
            s = k - nt3(ls, (lh[c2], ll[c2]))
            s = jnp.where(tile >= PANELS, s, 0.0)
            if c2 == 0:
                s = jnp.where(tile_c == 0, lf[:, :size], jnp.where(tile_c == 1, lf[:, size:], s))
            for half in range(size // 128):
                out[a, pl.ds(c2 * (size // 128) + half, size, stride=tile_cols * size // 128), :] = s[
                    :, half * 128 : half * 128 + 128
                ]


def per_device(points, rhs):
    rows_n = lax.axis_size("row")
    cols_n = lax.axis_size("col")
    tile_rows, _, size, feat = points.shape
    width = rhs.shape[-1]
    tile_cols = tile_rows * rows_n // cols_n
    pts = points[:, 0]
    right = rhs[:, 0].swapaxes(1, 2)
    jobs = 2 * PANELS + tile_cols
    any_spec = pl.BlockSpec(memory_space=pl.ANY)
    vmem = pl.BlockSpec(memory_space=pltpu.VMEM)
    piv, colp, rpiv = pl.pallas_call(
        functools.partial(fetch_kernel, rows_n, cols_n, tile_cols),
        out_shape=(
            jax.ShapeDtypeStruct((PANELS, size, feat), F32),
            jax.ShapeDtypeStruct((tile_cols, size, feat), F32),
            jax.ShapeDtypeStruct((PANELS, width, size), F32),
        ),
        in_specs=[any_spec] * 2,
        out_specs=(any_spec,) * 3,
        scratch_shapes=[
            pltpu.SemaphoreType.DMA((jobs, rows_n)),
            pltpu.SemaphoreType.DMA((jobs, 2)),
            pltpu.SemaphoreType.DMA((jobs,)),
        ],
        compiler_params=pltpu.CompilerParams(collective_id=0, has_side_effects=True),
        name="fetch",
    )(pts, right)
    factored, solved = pl.pallas_call(
        functools.partial(main_kernel, rows_n, cols_n),
        out_shape=(
            jax.ShapeDtypeStruct((tile_rows, size * tile_cols * size // 128, 128), F32),
            jax.ShapeDtypeStruct((tile_rows, width, size), F32),
        ),
        in_specs=[pl.BlockSpec(memory_space=pltpu.HBM)] * 5,
        out_specs=(vmem,) * 2,
        scratch_shapes=[
            pltpu.VMEM(pts.shape, F32),
            pltpu.VMEM(piv.shape, F32),
            pltpu.VMEM(colp.shape, F32),
            pltpu.VMEM(right.shape, F32),
            pltpu.VMEM(rpiv.shape, F32),
            pltpu.SemaphoreType.DMA((5,)),
            pltpu.VMEM((NB, 2 * NB), F32),
            pltpu.VMEM((size, 2 * size), F32),
            pltpu.VMEM((size, size), F32),
            pltpu.VMEM((size, size), F32),
            pltpu.VMEM((size, size), F32),
            pltpu.VMEM((size, 2 * size), F32),
            pltpu.VMEM((tile_cols, size, 2 * size), BF16),
            pltpu.VMEM((tile_cols, size, 2 * size), BF16),
            pltpu.VMEM((width, 2 * size), BF16),
            pltpu.VMEM((width, 2 * size), BF16),
        ],
        compiler_params=pltpu.CompilerParams(vmem_limit_bytes=62 * 1024 * 1024),
        name="panels",
    )(pts, piv, colp, right, rpiv)
    factored = factored.reshape(tile_rows, 1, size, tile_cols, 1, size)
    return factored, solved.swapaxes(1, 2)[:, None]


def solution(mesh):
    return jax.shard_map(
        per_device,
        mesh=mesh,
        in_specs=(P(None, "row", None, None), P(None, "row", None, "col")),
        out_specs=(P(None, "row", None, None, "col", None), P(None, "row", None, "col")),
        check_vma=False,
    )
```

profile of v0, /device:TPU:0, one launch (start us, length us, event | category | flops | bytes accessed | tf_op | source)
XLA Modules:
  0.0 53.6 jit_solution(16149760328389926029)
XLA Ops:
  0.6 17.4 %fetch.1 = (f32[2,256,128]{2,1,0:T(8,128)}, f32[2,256,128]{2,1,0:T(8,128)}, f32[2,32,256]{2,1,0:T(8,128)}) custom-call(f32[4,256,128]{2,1,0:T(8,128)} %bitcast.10, f32[4,32,256]{2,1,0:T(8,128)} %bitcast.12), custom_call_target="tpu_custom_call" | custom-call | tf_op jit(solution)/shard_map/fetch/pallas_call | solution.py:276
  18.0 35.4 %panels.1 = (f32[4,1024,128]{2,1,0:T(8,128)}, f32[4,32,256]{2,1,0:T(8,128)}) custom-call(f32[4,256,128]{2,1,0:T(8,128)} %bitcast.11, f32[2,256,128]{2,1,0:T(8,128)} %get-tuple-element.7.hpiv, f32[2,256,128]{2,1,0:T(8,128)} %get-tuple-element.8.hcolp, f32[4,32,256]{2,1,0:T(8,128)} %bitcast.13, f32[2,32,256]{2,1,0:T(8,128)} %get-tuple-element.9.hrpiv), custom_call_target="tpu_custom_call" | custom-call | tf_op jit(solution)/shard_map/panels/pallas_call | solution.py:293
where the time goes:
time: 53.7 us; the launch traced here: 53.6 us
  Pallas kernels  52.8 us (98%)
  between operations  0.8 us (1%)
    pallas_call x1, Pallas kernels, per_device(): pl.pallas_call(functools.partial(main_kernel, rows_n, cols_n), out_shape=...  35.4 us
    pallas_call x1, Pallas kernels, per_device(): pl.pallas_call(functools.partial(fetch_kernel, rows_n, cols_n, tile_cols)...  17.4 us

commit v1 on v0

v1 whole, which is shorter than its diff:
```python
import functools

import jax
import jax.numpy as jnp
from jax import lax
from jax.experimental import pallas as pl
from jax.experimental.pallas import tpu as pltpu
from jax.sharding import PartitionSpec as P

PANELS = 2
SCALE = 3.0
NUGGET = 1.0
HIGHEST = lax.Precision.HIGHEST
MESH = pl.DeviceIdType.MESH
F32 = jnp.float32
BF16 = jnp.bfloat16
NB = 128


def split(x):
    hi = x.astype(BF16)
    return hi, (x - hi.astype(F32)).astype(BF16)


def nt(a, b):
    return lax.dot_general(a, b, (((1,), (1,)), ((), ())), preferred_element_type=F32)


def nt3(a, b):
    return nt(a[0], b[0]) + (nt(a[0], b[1]) + nt(a[1], b[0]))


def squared_exp(a, b, b_sq):
    a_sq = jnp.sum(a * a, axis=1, keepdims=True)
    inner = nt3(split(a), split(b))
    return jnp.exp((-SCALE / a.shape[1]) * (a_sq + b_sq - 2.0 * inner))


def row_squares(b):
    ones = jnp.ones((8, b.shape[1]), F32)
    return lax.dot_general(
        ones, b * b, (((1,), (1,)), ((), ())), precision=HIGHEST, preferred_element_type=F32
    )[:1]


def spread(column):
    return jnp.broadcast_to(column, (column.shape[0], 2 * NB))


def base_inverse(block, base):
    eye = (
        lax.broadcasted_iota(jnp.int32, (NB, NB), 0) == lax.broadcasted_iota(jnp.int32, (NB, NB), 1)
    ).astype(F32)
    wide = jnp.concatenate([block, eye], axis=1)
    v = [wide[8 * q : 8 * q + 8] for q in range(NB // 8)]
    for j in range(0, NB, 4):
        q0, s = divmod(j, 8)
        cols = [[spread(v[q][:, j + n : j + n + 1]) for n in range(4)] for q in range(q0, NB // 8)]
        rows = [v[q0][s + n : s + n + 1] for n in range(4)]
        at = [[cols[0][n][s + m : s + m + 1] for n in range(4)] for m in range(4)]

        def pair(r0, r1, a, b, b1, c, where):
            det = a * c - b * b1
            inv_det = 1.0 / det
            e1 = a * r1 - b1 * r0
            rs = lax.rsqrt(a)
            base[where : where + 1, :] = r0 * rs
            base[where + 1 : where + 2, :] = e1 * (lax.rsqrt(det) * rs)
            return a, b, b1, c, inv_det, (c * r0 - b * r1) * inv_det, e1 * inv_det

        a, b, b1, c, inv_det, s0, s1 = pair(
            rows[0], rows[1], at[0][0], at[0][1], at[1][0], at[1][1], j
        )
        u0 = [(c * at[0][n] - b * at[1][n]) * inv_det for n in (2, 3)]
        u1 = [(a * at[1][n] - b1 * at[0][n]) * inv_det for n in (2, 3)]
        r2, r3 = (rows[m] - at[m][0] * s0 - at[m][1] * s1 for m in (2, 3))
        p = [[at[m][n + 2] - at[m][0] * u0[n] - at[m][1] * u1[n] for n in (0, 1)] for m in (2, 3)]
        s2, s3 = pair(r2, r3, p[0][0], p[0][1], p[1][0], p[1][1], j + 2)[5:]
        for q in range(q0 if s == 0 else q0 + 1, NB // 8):
            k0, k1, k2, k3 = cols[q - q0]
            k2 = k2 - k0 * u0[0] - k1 * u1[0]
            k3 = k3 - k0 * u0[1] - k1 * u1[1]
            v[q] = v[q] - k0 * s0 - k1 * s1 - k2 * s2 - k3 * s3
    return base[:, NB:]


def inverse_factor(w, h, base):
    size = h.shape[0]
    for j0 in range(0, size, NB):
        j1 = j0 + NB
        inv = base_inverse(w[j0:j1, j0:j1], base)
        rows = jnp.dot(inv, w[j0:j1, :], precision=HIGHEST, preferred_element_type=F32)
        h[j0:j1, :] = rows[:, size:]
        if j1 < size:
            panel = lax.dot_general(
                w[j1:, j0:j1], inv, (((1,), (1,)), ((), ())), precision=HIGHEST, preferred_element_type=F32
            )
            w[j1:, :] = w[j1:, :] - jnp.dot(
                panel, rows, precision=HIGHEST, preferred_element_type=F32
            )


def factor_kernel(
    rows_n, cols_n, tile_cols, pts, prhs, opiv, ocolp, oh, oy,
    piv, colp, rpiv, base, w, h0, h1, hs, ys, send, recv, local, wsem,
):
    row_id = lax.axis_index("row")
    col_id = lax.axis_index("col")
    stride = cols_n // rows_n

    barrier = pltpu.get_barrier_semaphore()
    for step in range(1, rows_n):
        other = lax.rem(row_id + step, rows_n)
        pl.semaphore_signal(barrier, inc=1, device_id={"row": other}, device_id_type=MESH)

    jobs = [(k % rows_n, pts.at[k // rows_n], piv.at[k]) for k in range(PANELS)]
    jobs += [(k % rows_n, prhs.at[k // rows_n], rpiv.at[k]) for k in range(PANELS)]
    for c2 in range(tile_cols):
        slot = c2 * stride + col_id // rows_n
        jobs.append((lax.rem(col_id, rows_n), pts.at[slot], colp.at[c2]))

    chips = rows_n // 2
    chip, core = row_id // 2, lax.rem(row_id, 2)
    sibling = row_id + 1 - 2 * core

    def half_of(ref, half):
        height = ref.shape[0] // 2
        return ref.at[pl.ds(pl.multiple_of(half * height, height), height)]

    def remote(number, half, dest, slot, relay=False):
        _, src, dst = jobs[number]
        return pltpu.make_async_remote_copy(
            src_ref=half_of(dst if relay else src, half),
            dst_ref=half_of(dst, half),
            send_sem=send.at[number, slot],
            recv_sem=recv.at[number, half],
            device_id={"row": dest},
            device_id_type=MESH,
        )

    def sends(number):
        out = []
        for step in range(1, chips):
            for half in range(2):
                dest = 2 * lax.rem(chip + step, chips) + half
                out.append(remote(number, half, dest, 2 * step + half))
        return out + [remote(number, half, sibling, half) for half in range(2)]

    def own(number):
        _, src, dst = jobs[number]
        return pltpu.make_async_copy(src, dst, local.at[number])

    def when(condition):
        return pl.when(condition)

    def launch(number):
        @when(row_id == jobs[number][0])
        def _():
            for copy in sends(number):
                copy.start()

    def relay(number):
        @when(chip != jobs[number][0] // 2)
        def _():
            copy = remote(number, core, sibling, 0, relay=True)
            copy.wait_recv()
            copy.start()

    def arrive(number):
        owner = jobs[number][0]

        @when(row_id == owner)
        def _():
            own(number).wait()

        @when(sibling == owner)
        def _():
            for half in range(2):
                remote(number, half, sibling, half).wait_recv()

        @when(chip != owner // 2)
        def _():
            remote(number, 1 - core, sibling, 0, relay=True).wait_recv()

    def drain(number):
        owner = jobs[number][0]

        @when(row_id == owner)
        def _():
            for copy in sends(number):
                copy.wait_send()

        @when(chip != owner // 2)
        def _():
            remote(number, core, sibling, 0, relay=True).wait_send()

    for number in range(len(jobs)):
        @when(row_id == jobs[number][0])
        def _(number=number):
            own(number).start()

    pl.semaphore_wait(barrier, rows_n - 1)
    for number in range(len(jobs)):
        launch(number)
    relay(0)
    arrive(0)

    size = piv.shape[1]
    eye = (
        lax.broadcasted_iota(jnp.int32, (size, size), 0) == lax.broadcasted_iota(jnp.int32, (size, size), 1)
    ).astype(F32)
    x0 = piv[0]
    sq0 = row_squares(x0)
    w[:, :size] = squared_exp(x0, x0, sq0) + NUGGET * eye
    w[:, size:] = eye
    inverse_factor(w, h0, base)

    for number in range(1, len(jobs)):
        relay(number)
    for number in range(1, len(jobs)):
        arrive(number)
    writes = [pltpu.make_async_copy(piv, opiv, wsem.at[0]), pltpu.make_async_copy(colp, ocolp, wsem.at[1])]
    for copy in writes:
        copy.start()

    x1 = piv[1]
    sq1 = row_squares(x1)
    h0s = split(h0[...])
    hs[0, 0], hs[0, 1] = h0s
    l10s = split(nt3(split(squared_exp(x1, x0, sq0)), h0s))
    w[:, :size] = squared_exp(x1, x1, sq1) + NUGGET * eye - nt3(l10s, l10s)
    w[:, size:] = eye
    inverse_factor(w, h1, base)
    h1s = split(h1[...])
    hs[1, 0], hs[1, 1] = h1s
    hx = -nn3(split(nn3(h1s, l10s)), h0s)
    hxs = split(hx)
    hs[2, 0], hs[2, 1] = hxs
    writes.append(pltpu.make_async_copy(hs, oh, wsem.at[2]))
    writes[-1].start()
    r0, r1 = split(rpiv[0]), split(rpiv[1])
    ys[:, :size] = nt3(r0, h0s)
    ys[:, size:] = nt3(r0, hxs) + nt3(r1, h1s)
    writes.append(pltpu.make_async_copy(ys, oy, wsem.at[3]))
    writes[-1].start()
    for number in range(len(jobs)):
        drain(number)
    for copy in writes:
        copy.wait()


def nn(a, b):
    return lax.dot_general(a, b, (((1,), (0,)), ((), ())), preferred_element_type=F32)


def nn3(a, b):
    return nn(a[0], b[0]) + (nn(a[0], b[1]) + nn(a[1], b[0]))


def tiles_kernel(
    rows_n, cols_n, hpts, hpiv, hcolp, hrhs, hh, hy, out, solved,
    pts, piv, colp, rhs, hs, ys, lh, ll, stage, rest, sems, osems,
):
    row_id = lax.axis_index("row")
    col_id = lax.axis_index("col")
    copies = [
        pltpu.make_async_copy(src, dst, sems.at[n])
        for n, (src, dst) in enumerate(
            ((hpiv, piv), (hcolp, colp), (hh, hs), (hpts, pts), (hrhs, rhs), (hy, ys))
        )
    ]
    for copy in copies:
        copy.start()
    tile_rows, size, _ = pts.shape
    tile_cols = colp.shape[0]
    row_in = lax.broadcasted_iota(jnp.int32, (size, size), 0)
    col_in = lax.broadcasted_iota(jnp.int32, (size, size), 1)
    eye = (row_in == col_in).astype(F32)
    lower = row_in >= col_in
    for copy in copies:
        copy.wait()
    x0, x1 = piv[0], piv[1]
    sq0, sq1 = row_squares(x0), row_squares(x1)
    h0s, h1s, hxs = ((hs[n, 0], hs[n, 1]) for n in range(3))

    def panels_of(x, tile):
        k0 = split(squared_exp(x, x0, sq0) + jnp.where(tile == 0, NUGGET, 0.0) * eye)
        l0 = nt3(k0, h0s)
        l0 = jnp.where((tile != 0) | lower, l0, 0.0)
        k1 = split(squared_exp(x, x1, sq1) + jnp.where(tile == 1, NUGGET, 0.0) * eye)
        l1 = nt3(k0, hxs) + nt3(k1, h1s)
        l1 = jnp.where((tile > 1) | (lower & (tile == 1)), l1, 0.0)
        return l0, l1

    for c2 in range(tile_cols):
        l0, l1 = panels_of(colp[c2], c2 * cols_n + col_id)
        lh[c2, :, :size], ll[c2, :, :size] = split(l0)
        lh[c2, :, size:], ll[c2, :, size:] = split(l1)
    yv = ys[...]
    y = split(yv)

    writes = []
    for a in range(tile_rows):
        tile = a * rows_n + row_id
        x = pts[a]
        l0, l1 = panels_of(x, tile)
        ls = split(jnp.concatenate([l0, l1], axis=1))
        left = rhs[a] - nt3(y, ls)
        rest[a] = jnp.where(tile == 0, yv[:, :size], jnp.where(tile == 1, yv[:, size:], left))
        for c2 in range(tile_cols):
            tile_c = c2 * cols_n + col_id
            xc = colp[c2]
            k = squared_exp(x, xc, row_squares(xc)) + jnp.where(tile == tile_c, NUGGET, 0.0) * eye
            s = k - nt3(ls, (lh[c2], ll[c2]))
            s = jnp.where(tile >= PANELS, s, 0.0)
            if c2 == 0:
                s = jnp.where(tile_c == 0, l0, jnp.where(tile_c == 1, l1, s))
            for half in range(size // 128):
                stage[a, pl.ds(c2 * (size // 128) + half, size, stride=tile_cols * size // 128), :] = s[
                    :, half * 128 : half * 128 + 128
                ]
        writes.append(pltpu.make_async_copy(stage.at[a], out.at[a], osems.at[a]))
        writes[-1].start()
    writes.append(pltpu.make_async_copy(rest, solved, osems.at[tile_rows]))
    writes[-1].start()
    for copy in writes:
        copy.wait()


def per_device(points, rhs):
    rows_n = lax.axis_size("row")
    cols_n = lax.axis_size("col")
    tile_rows, _, size, feat = points.shape
    width = rhs.shape[-1]
    tile_cols = tile_rows * rows_n // cols_n
    pts = points[:, 0]
    right = rhs[:, 0].swapaxes(1, 2)
    jobs = 2 * PANELS + tile_cols
    hbm = pl.BlockSpec(memory_space=pltpu.HBM)
    piv_s, colp_s = (PANELS, size, feat), (tile_cols, size, feat)
    h_s, y_s = (3, 2, size, size), (width, PANELS * size)
    piv, colp, hs, ys = pl.pallas_call(
        functools.partial(factor_kernel, rows_n, cols_n, tile_cols),
        out_shape=(
            jax.ShapeDtypeStruct(piv_s, F32),
            jax.ShapeDtypeStruct(colp_s, F32),
            jax.ShapeDtypeStruct(h_s, BF16),
            jax.ShapeDtypeStruct(y_s, F32),
        ),
        in_specs=[hbm] * 2,
        out_specs=(hbm,) * 4,
        scratch_shapes=[
            pltpu.VMEM(piv_s, F32),
            pltpu.VMEM(colp_s, F32),
            pltpu.VMEM((PANELS, width, size), F32),
            pltpu.VMEM((NB, 2 * NB), F32),
            pltpu.VMEM((size, 2 * size), F32),
            pltpu.VMEM((size, size), F32),
            pltpu.VMEM((size, size), F32),
            pltpu.VMEM(h_s, BF16),
            pltpu.VMEM(y_s, F32),
            pltpu.SemaphoreType.DMA((jobs, rows_n)),
            pltpu.SemaphoreType.DMA((jobs, 2)),
            pltpu.SemaphoreType.DMA((jobs,)),
            pltpu.SemaphoreType.DMA((4,)),
        ],
        compiler_params=pltpu.CompilerParams(
            collective_id=0, has_side_effects=True, vmem_limit_bytes=62 * 1024 * 1024
        ),
        name="factor",
    )(pts, right)
    out_s = (tile_rows, size * tile_cols * size // 128, 128)
    factored, solved = pl.pallas_call(
        functools.partial(tiles_kernel, rows_n, cols_n),
        out_shape=(
            jax.ShapeDtypeStruct(out_s, F32),
            jax.ShapeDtypeStruct((tile_rows, width, size), F32),
        ),
        in_specs=[hbm] * 6,
        out_specs=(hbm,) * 2,
        scratch_shapes=[
            pltpu.VMEM(pts.shape, F32),
            pltpu.VMEM(piv_s, F32),
            pltpu.VMEM(colp_s, F32),
            pltpu.VMEM(right.shape, F32),
            pltpu.VMEM(h_s, BF16),
            pltpu.VMEM(y_s, F32),
            pltpu.VMEM((tile_cols, size, PANELS * size), BF16),
            pltpu.VMEM((tile_cols, size, PANELS * size), BF16),
            pltpu.VMEM(out_s, F32),
            pltpu.VMEM((tile_rows, width, size), F32),
            pltpu.SemaphoreType.DMA((6,)),
            pltpu.SemaphoreType.DMA((tile_rows + 1,)),
        ],
        compiler_params=pltpu.CompilerParams(vmem_limit_bytes=62 * 1024 * 1024),
        name="tiles",
    )(pts, piv, colp, right, hs, ys)
    factored = factored.reshape(tile_rows, 1, size, tile_cols, 1, size)
    return factored, solved.swapaxes(1, 2)[:, None]


def solution(mesh):
    return jax.shard_map(
        per_device,
        mesh=mesh,
        in_specs=(P(None, "row", None, None), P(None, "row", None, "col")),
        out_specs=(P(None, "row", None, None, "col", None), P(None, "row", None, "col")),
        check_vma=False,
    )
```

time: 53.7 us -> 44.7 us (0.83)
  the two profiles are of different devices: /device:TPU:0 before, /device:TPU:29 now
where the time goes in v1:
time: 44.7 us; the launch traced here: 44 us
  Pallas kernels  43.2 us (97%)
  between operations  0.8 us (2%)
    pallas_call x1, Pallas kernels, per_device(): pl.pallas_call(functools.partial(factor_kernel, rows_n, cols_n, tile_cols...  31.2 us
    pallas_call x1, Pallas kernels, per_device(): pl.pallas_call(functools.partial(tiles_kernel, rows_n, cols_n), out_shape...  11.9 us

profile of v1, /device:TPU:29, one launch (start us, length us, event | category | flops | bytes accessed | tf_op | source)
XLA Modules:
  0.0 44.0 jit_solution(7116649771455188699)
XLA Ops:
  0.6 31.2 %factor.1 = (f32[2,256,128]{2,1,0:T(8,128)}, f32[2,256,128]{2,1,0:T(8,128)}, bf16[3,2,256,256]{3,2,1,0:T(8,128)(2,1)}, f32[32,512]{1,0:T(8,128)}) custom-call(f32[4,256,128]{2,1,0:T(8,128)} %bitcast.10, f32[4,32,256]{2,1,0:T(8,128)} %bitcast.12), custom_call_target="tpu_custom_call" | custom-call | tf_op jit(solution)/shard_map/factor/pallas_call | solution.py:342
  31.9 11.9 %tiles.1 = (f32[4,1024,128]{2,1,0:T(8,128)}, f32[4,32,256]{2,1,0:T(8,128)}) custom-call(f32[4,256,128]{2,1,0:T(8,128)} %bitcast.11, f32[2,256,128]{2,1,0:T(8,128)} %get-tuple-element.8.hpiv, f32[2,256,128]{2,1,0:T(8,128)} %get-tuple-element.9.hcolp, f32[4,32,256]{2,1,0:T(8,128)} %bitcast.13, bf16[3,2,256,256]{3,2,1,0:T(8,128)(2,1)} %get-tuple-element.10.hh, ...), custom_call_target="tpu_custom_call" | custom-call | tf_op jit(solution)/shard_map/tiles/pallas_call | solution.py:373

commit v2 on v1

--- a/solution.py
+++ b/solution.py
@@ -43,66 +43,91 @@
     )[:1]
 
 
-def spread(column):
-    return jnp.broadcast_to(column, (column.shape[0], 2 * NB))
-
-
-def base_inverse(block, base):
-    eye = (
-        lax.broadcasted_iota(jnp.int32, (NB, NB), 0) == lax.broadcasted_iota(jnp.int32, (NB, NB), 1)
-    ).astype(F32)
-    wide = jnp.concatenate([block, eye], axis=1)
-    v = [wide[8 * q : 8 * q + 8] for q in range(NB // 8)]
-    for j in range(0, NB, 4):
-        q0, s = divmod(j, 8)
-        cols = [[spread(v[q][:, j + n : j + n + 1]) for n in range(4)] for q in range(q0, NB // 8)]
-        rows = [v[q0][s + n : s + n + 1] for n in range(4)]
-        at = [[cols[0][n][s + m : s + m + 1] for n in range(4)] for m in range(4)]
-
-        def pair(r0, r1, a, b, b1, c, where):
-            det = a * c - b * b1
-            inv_det = 1.0 / det
-            e1 = a * r1 - b1 * r0
+def splat(tile, j):
+    return jnp.broadcast_to(tile[:, j:j+1], tile.shape)
+def rowof(tile, s):
+    return jnp.broadcast_to(tile[s:s+1], tile.shape)
+
+def base_inverse(block, width=16, ahead=2):
+    lane = lax.broadcasted_iota(jnp.int32, (8, NB), 1)
+    sub = lax.broadcasted_iota(jnp.int32, (8, NB), 0)
+    v = [block[8 * q : 8 * q + 8] for q in range(NB // 8)]
+    rows_n = len(v)
+    per = width // 8
+    out = []
+    for j in range(0, NB, width):
+        q0 = j // 8
+        near = list(range(q0 + per, min(q0 + per + ahead, rows_n)))
+        far = list(range(q0 + per + ahead, rows_n))
+        d = [[splat(v[q0+t], j+n) for n in range(width)] for t in range(per)]
+        d[0] = [jnp.where(lane >= 0, x, 0.0) for x in d[0]]
+        low = [[splat(v[q], j+n) for n in range(width)] for q in near]
+        inside = (lane >= j) & (lane < j+width)
+        r = [jnp.where(inside, (lane - j == sub + 8*t).astype(F32), v[q0+t]) for t in range(per)]
+        f = [None]*per
+        S = [None]*width
+        us = {}
+        for n in range(0, width, 2):
+            t, s = divmod(n, 8)
+            a, b, c = rowof(d[t][n], s), rowof(d[t][n+1], s), rowof(d[t][n+1], s+1)
+            det = a*c - b*b
+            inv = 1.0/det
+            ai, bi, ci = a*inv, b*inv, c*inv
+            r0, r1 = rowof(r[t], s), rowof(r[t], s+1)
             rs = lax.rsqrt(a)
-            base[where : where + 1, :] = r0 * rs
-            base[where + 1 : where + 2, :] = e1 * (lax.rsqrt(det) * rs)
-            return a, b, b1, c, inv_det, (c * r0 - b * r1) * inv_det, e1 * inv_det
-
-        a, b, b1, c, inv_det, s0, s1 = pair(
-            rows[0], rows[1], at[0][0], at[0][1], at[1][0], at[1][1], j
-        )
-        u0 = [(c * at[0][n] - b * at[1][n]) * inv_det for n in (2, 3)]
-        u1 = [(a * at[1][n] - b1 * at[0][n]) * inv_det for n in (2, 3)]
-        r2, r3 = (rows[m] - at[m][0] * s0 - at[m][1] * s1 for m in (2, 3))
-        p = [[at[m][n + 2] - at[m][0] * u0[n] - at[m][1] * u1[n] for n in (0, 1)] for m in (2, 3)]
-        s2, s3 = pair(r2, r3, p[0][0], p[0][1], p[1][0], p[1][1], j + 2)[5:]
-        for q in range(q0 if s == 0 else q0 + 1, NB // 8):
-            k0, k1, k2, k3 = cols[q - q0]
-            k2 = k2 - k0 * u0[0] - k1 * u1[0]
-            k3 = k3 - k0 * u0[1] - k1 * u1[1]
-            v[q] = v[q] - k0 * s0 - k1 * s1 - k2 * s2 - k3 * s3
-    return base[:, NB:]
-
-
-def inverse_factor(w, h, base):
-    size = h.shape[0]
-    for j0 in range(0, size, NB):
-        j1 = j0 + NB
-        inv = base_inverse(w[j0:j1, j0:j1], base)
-        rows = jnp.dot(inv, w[j0:j1, :], precision=HIGHEST, preferred_element_type=F32)
-        h[j0:j1, :] = rows[:, size:]
-        if j1 < size:
-            panel = lax.dot_general(
-                w[j1:, j0:j1], inv, (((1,), (1,)), ((), ())), precision=HIGHEST, preferred_element_type=F32
-            )
-            w[j1:, :] = w[j1:, :] - jnp.dot(
-                panel, rows, precision=HIGHEST, preferred_element_type=F32
-            )
+            f0 = r0*rs
+            f1 = (a*r1 - b*r0)*(lax.rsqrt(det)*rs)
+            f[t] = f0 if f[t] is None else jnp.where(sub == s, f0, f[t])
+            f[t] = jnp.where(sub == s+1, f1, f[t])
+            S[n], S[n+1] = ci*r0 - bi*r1, ai*r1 - bi*r0
+            for m in range(n+2, width):
+                x, y = rowof(d[t][m], s), rowof(d[t][m], s+1)
+                u0, u1 = ci*x - bi*y, ai*y - bi*x
+                us[n, m] = u0, u1
+                for tt in range((n+2)//8, per):
+                    d[tt][m] = d[tt][m] - (d[tt][n]*u0 + d[tt][n+1]*u1)
+            for tt in range((n+2)//8, per):
+                r[tt] = r[tt] - (d[tt][n]*S[n] + d[tt][n+1]*S[n+1])
+        if near:
+            for n in range(width-4, -1, -2):
+                for m in range(width-1, n+1, -1):
+                    u0, u1 = us[n, m]
+                    S[n] = S[n] - u0*S[m]
+                    S[n+1] = S[n+1] - u1*S[m]
+        for t in range(per):
+            out.append(jnp.where(lane <= j + 8*t + sub, f[t], 0.0))
+        for i, q in enumerate(near):
+            acc = [low[i][n]*S[n] for n in range(4)]
+            for n in range(4, width):
+                acc[n % 4] = acc[n % 4] + low[i][n]*S[n]
+            v[q] = jnp.where(inside, 0.0, v[q]) - ((acc[0]+acc[1])+(acc[2]+acc[3]))
+        if far:
+            fc = jnp.concatenate(f, axis=0)
+            hi = fc.astype(BF16)
+            lo = (fc - hi.astype(F32)).astype(BF16)
+            up = lax.dot_general(jnp.concatenate([hi, hi, lo], axis=0), jnp.concatenate([hi, lo, hi], axis=0),
+                                 (((0,), (0,)), ((), ())), preferred_element_type=F32)
+            for q in far:
+                v[q] = jnp.where(inside, 0.0, v[q]) - up[8*q:8*q+8]
+    return jnp.concatenate(out, axis=0)
+
+
+def inverse_factor(w, h):
+    inv = base_inverse(w[:NB, :NB])
+    h[:NB, :NB] = inv
+    h[:NB, NB:] = jnp.zeros((NB, w.shape[1] - NB), F32)
+    first = split(inv)
+    below = split(nt3(split(w[NB:, :NB]), first))
+    w[NB:, NB:] = w[NB:, NB:] - nt3(below, below)
+    mixed = split(nn3(below, first))
+    inv = base_inverse(w[NB:, NB:])
+    h[NB:, NB:] = inv
+    h[NB:, :NB] = -nn3(split(inv), mixed)
 
 
 def factor_kernel(
     rows_n, cols_n, tile_cols, pts, prhs, opiv, ocolp, oh, oy,
-    piv, colp, rpiv, base, w, h0, h1, hs, ys, send, recv, local, wsem,
+    piv, colp, rpiv, w, h0, h1, hs, ys, send, recv, local, wsem,
 ):
     row_id = lax.axis_index("row")
     col_id = lax.axis_index("col")
@@ -185,10 +210,11 @@
     def drain(number):
         owner = jobs[number][0]
 
-        @when(row_id == owner)
-        def _():
-            for copy in sends(number):
-                copy.wait_send()
+        if number:
+            @when(row_id == owner)
+            def _():
+                for copy in sends(number):
+                    copy.wait_send()
 
         @when(chip != owner // 2)
         def _():
@@ -200,10 +226,17 @@
             own(number).start()
 
     pl.semaphore_wait(barrier, rows_n - 1)
-    for number in range(len(jobs)):
-        launch(number)
+    launch(0)
     relay(0)
     arrive(0)
+
+    @when(row_id == jobs[0][0])
+    def _():
+        for copy in sends(0):
+            copy.wait_send()
+
+    for number in range(1, len(jobs)):
+        launch(number)
 
     size = piv.shape[1]
     eye = (
@@ -211,30 +244,29 @@
     ).astype(F32)
     x0 = piv[0]
     sq0 = row_squares(x0)
-    w[:, :size] = squared_exp(x0, x0, sq0) + NUGGET * eye
-    w[:, size:] = eye
-    inverse_factor(w, h0, base)
+    w[...] = squared_exp(x0, x0, sq0) + NUGGET * eye
+    inverse_factor(w, h0)
+    h0s = split(h0[...])
+    hs[0, 0], hs[0, 1] = h0s
 
     for number in range(1, len(jobs)):
         relay(number)
-    for number in range(1, len(jobs)):
+    arrive(1)
+    x1 = piv[1]
+    sq1 = row_squares(x1)
+    l10s = split(nt3(split(squared_exp(x1, x0, sq0)), h0s))
+    w[...] = squared_exp(x1, x1, sq1) + NUGGET * eye - nt3(l10s, l10s)
+    mixed = split(nn3(l10s, h0s))
+    inverse_factor(w, h1)
+
+    for number in range(2, len(jobs)):
         arrive(number)
     writes = [pltpu.make_async_copy(piv, opiv, wsem.at[0]), pltpu.make_async_copy(colp, ocolp, wsem.at[1])]
     for copy in writes:
         copy.start()
-
-    x1 = piv[1]
-    sq1 = row_squares(x1)
-    h0s = split(h0[...])
-    hs[0, 0], hs[0, 1] = h0s
-    l10s = split(nt3(split(squared_exp(x1, x0, sq0)), h0s))
-    w[:, :size] = squared_exp(x1, x1, sq1) + NUGGET * eye - nt3(l10s, l10s)
-    w[:, size:] = eye
-    inverse_factor(w, h1, base)
     h1s = split(h1[...])
     hs[1, 0], hs[1, 1] = h1s
-    hx = -nn3(split(nn3(h1s, l10s)), h0s)
-    hxs = split(hx)
+    hxs = split(-nn3(h1s, mixed))
     hs[2, 0], hs[2, 1] = hxs
     writes.append(pltpu.make_async_copy(hs, oh, wsem.at[2]))
     writes[-1].start()
@@ -353,8 +385,7 @@
             pltpu.VMEM(piv_s, F32),
             pltpu.VMEM(colp_s, F32),
             pltpu.VMEM((PANELS, width, size), F32),
-            pltpu.VMEM((NB, 2 * NB), F32),
-            pltpu.VMEM((size, 2 * size), F32),
+            pltpu.VMEM((size, size), F32),
             pltpu.VMEM((size, size), F32),
             pltpu.VMEM((size, size), F32),
             pltpu.VMEM(h_s, BF16),

time: 44.7 us -> 35.5 us (0.79); the launches traced: 44 us -> 35.3 us
  Pallas kernels: 43.2 us -> 34.5 us
    pallas_call x1, Pallas kernels: 31.2 us -> 22.4 us  [per_device(): pl.pallas_call(functools.partial(factor_kernel, rows_n, cols_n, tile_cols...]
where the time goes in v2:
time: 35.5 us; the launch traced here: 35.3 us
  Pallas kernels  34.5 us (97%)
  between operations  0.8 us (2%)
    pallas_call x1, Pallas kernels, per_device(): pl.pallas_call(functools.partial(factor_kernel, rows_n, cols_n, tile_cols...  22.4 us
    pallas_call x1, Pallas kernels, per_device(): pl.pallas_call(functools.partial(tiles_kernel, rows_n, cols_n), out_shape...  12.1 us

profile of v2, /device:TPU:29, one launch (start us, length us, event | category | flops | bytes accessed | tf_op | source)
XLA Modules:
  0.0 35.3 jit_solution(18302880853184168683)
XLA Ops:
  0.6 22.4 %factor.1 = (f32[2,256,128]{2,1,0:T(8,128)}, f32[2,256,128]{2,1,0:T(8,128)}, bf16[3,2,256,256]{3,2,1,0:T(8,128)(2,1)}, f32[32,512]{1,0:T(8,128)}) custom-call(f32[4,256,128]{2,1,0:T(8,128)} %bitcast.10, f32[4,32,256]{2,1,0:T(8,128)} %bitcast.12), custom_call_target="tpu_custom_call" | custom-call | tf_op jit(solution)/shard_map/factor/pallas_call | solution.py:374
  23.0 12.1 %tiles.1 = (f32[4,1024,128]{2,1,0:T(8,128)}, f32[4,32,256]{2,1,0:T(8,128)}) custom-call(f32[4,256,128]{2,1,0:T(8,128)} %bitcast.11, f32[2,256,128]{2,1,0:T(8,128)} %get-tuple-element.8.hpiv, f32[2,256,128]{2,1,0:T(8,128)} %get-tuple-element.9.hcolp, f32[4,32,256]{2,1,0:T(8,128)} %bitcast.13, bf16[3,2,256,256]{3,2,1,0:T(8,128)(2,1)} %get-tuple-element.10.hh, ...), custom_call_target="tpu_custom_call" | custom-call | tf_op jit(solution)/shard_map/tiles/pallas_call | solution.py:404

commit v3 on v2

--- a/solution.py
+++ b/solution.py
@@ -15,6 +15,7 @@
 F32 = jnp.float32
 BF16 = jnp.bfloat16
 NB = 128
+LOG2E = 1.4426950408889634
 
 
 def split(x):
@@ -112,8 +113,7 @@
     return jnp.concatenate(out, axis=0)
 
 
-def inverse_factor(w, h):
-    inv = base_inverse(w[:NB, :NB])
+def inverse_factor(w, h, inv):
     h[:NB, :NB] = inv
     h[:NB, NB:] = jnp.zeros((NB, w.shape[1] - NB), F32)
     first = split(inv)
@@ -138,7 +138,8 @@
         other = lax.rem(row_id + step, rows_n)
         pl.semaphore_signal(barrier, inc=1, device_id={"row": other}, device_id_type=MESH)
 
-    jobs = [(k % rows_n, pts.at[k // rows_n], piv.at[k]) for k in range(PANELS)]
+    jobs = [(0, pts.at[0, pl.ds(n * NB, NB)], piv.at[0, pl.ds(n * NB, NB)]) for n in range(2)]
+    jobs += [(k % rows_n, pts.at[k // rows_n], piv.at[k]) for k in range(1, PANELS)]
     jobs += [(k % rows_n, prhs.at[k // rows_n], rpiv.at[k]) for k in range(PANELS)]
     for c2 in range(tile_cols):
         slot = c2 * stride + col_id // rows_n
@@ -154,6 +155,15 @@
 
     def remote(number, half, dest, slot, relay=False):
         _, src, dst = jobs[number]
+        if number == 1:
+            return pltpu.make_async_remote_copy(
+                src_ref=src,
+                dst_ref=dst,
+                send_sem=send.at[number, slot],
+                recv_sem=recv.at[number, 0],
+                device_id={"row": dest},
+                device_id_type=MESH,
+            )
         return pltpu.make_async_remote_copy(
             src_ref=half_of(dst if relay else src, half),
             dst_ref=half_of(dst, half),
@@ -169,7 +179,7 @@
             for half in range(2):
                 dest = 2 * lax.rem(chip + step, chips) + half
                 out.append(remote(number, half, dest, 2 * step + half))
-        return out + [remote(number, half, sibling, half) for half in range(2)]
+        return out + [remote(number, half, sibling, half) for half in range(1 if number == 1 else 2)]
 
     def own(number):
         _, src, dst = jobs[number]
@@ -210,11 +220,10 @@
     def drain(number):
         owner = jobs[number][0]
 
-        if number:
-            @when(row_id == owner)
-            def _():
-                for copy in sends(number):
-                    copy.wait_send()
+        @when(row_id == owner)
+        def _():
+            for copy in sends(number):
+                copy.wait_send()
 
         @when(chip != owner // 2)
         def _():
@@ -229,12 +238,7 @@
     launch(0)
     relay(0)
     arrive(0)
-
-    @when(row_id == jobs[0][0])
-    def _():
-        for copy in sends(0):
-            copy.wait_send()
-
+    drain(0)
     for number in range(1, len(jobs)):
         launch(number)
 
@@ -242,32 +246,48 @@
     eye = (
         lax.broadcasted_iota(jnp.int32, (size, size), 0) == lax.broadcasted_iota(jnp.int32, (size, size), 1)
     ).astype(F32)
+    xa = piv[0, :NB]
+    sqa = row_squares(xa)
+    w[:NB, :NB] = squared_exp(xa, xa, sqa) + NUGGET * eye[:NB, :NB]
+    inv = base_inverse(w[:NB, :NB])
+
+    @when(row_id == 0)
+    def _():
+        own(1).wait()
+
+    @when(row_id != 0)
+    def _():
+        remote(1, 0, 0, 0).wait_recv()
+
+    xb = piv[0, NB:]
+    w[NB:, :NB] = squared_exp(xb, xa, sqa)
+    w[NB:, NB:] = squared_exp(xb, xb, row_squares(xb)) + NUGGET * eye[:NB, :NB]
+    inverse_factor(w, h0, inv)
     x0 = piv[0]
     sq0 = row_squares(x0)
-    w[...] = squared_exp(x0, x0, sq0) + NUGGET * eye
-    inverse_factor(w, h0)
     h0s = split(h0[...])
-    hs[0, 0], hs[0, 1] = h0s
-
-    for number in range(1, len(jobs)):
+    hs[:, : 3 * size] = right3(h0[...])
+
+    for number in range(2, len(jobs)):
         relay(number)
-    arrive(1)
+    arrive(2)
     x1 = piv[1]
     sq1 = row_squares(x1)
     l10s = split(nt3(split(squared_exp(x1, x0, sq0)), h0s))
     w[...] = squared_exp(x1, x1, sq1) + NUGGET * eye - nt3(l10s, l10s)
     mixed = split(nn3(l10s, h0s))
-    inverse_factor(w, h1)
-
-    for number in range(2, len(jobs)):
+    inverse_factor(w, h1, base_inverse(w[:NB, :NB]))
+
+    for number in range(3, len(jobs)):
         arrive(number)
     writes = [pltpu.make_async_copy(piv, opiv, wsem.at[0]), pltpu.make_async_copy(colp, ocolp, wsem.at[1])]
     for copy in writes:
         copy.start()
     h1s = split(h1[...])
-    hs[1, 0], hs[1, 1] = h1s
-    hxs = split(-nn3(h1s, mixed))
-    hs[2, 0], hs[2, 1] = hxs
+    hx = -nn3(h1s, mixed)
+    hxs = split(hx)
+    hs[:, 3 * size : 6 * size] = right3(hx)
+    hs[:, 6 * size :] = right3(h1[...])
     writes.append(pltpu.make_async_copy(hs, oh, wsem.at[2]))
     writes[-1].start()
     r0, r1 = split(rpiv[0]), split(rpiv[1])
@@ -275,7 +295,12 @@
     ys[:, size:] = nt3(r0, hxs) + nt3(r1, h1s)
     writes.append(pltpu.make_async_copy(ys, oy, wsem.at[3]))
     writes[-1].start()
-    for number in range(len(jobs)):
+    @when(row_id == 0)
+    def _():
+        for copy in sends(1):
+            copy.wait_send()
+
+    for number in range(2, len(jobs)):
         drain(number)
     for copy in writes:
         copy.wait()
@@ -289,72 +314,134 @@
     return nn(a[0], b[0]) + (nn(a[0], b[1]) + nn(a[1], b[0]))
 
 
+def left3(x):
+    hi, lo = split(x)
+    return jnp.concatenate([hi, hi, lo], axis=1)
+
+
+def right3(x):
+    hi, lo = split(x)
+    return jnp.concatenate([hi, lo, hi], axis=1)
+
+
 def tiles_kernel(
     rows_n, cols_n, hpts, hpiv, hcolp, hrhs, hh, hy, out, solved,
-    pts, piv, colp, rhs, hs, ys, lh, ll, stage, rest, sems, osems,
+    pts, piv, colp, rhs, hs, ys, k3, lr3, lc3, stage, rest, sems, osems,
 ):
     row_id = lax.axis_index("row")
     col_id = lax.axis_index("col")
     copies = [
         pltpu.make_async_copy(src, dst, sems.at[n])
         for n, (src, dst) in enumerate(
-            ((hpiv, piv), (hcolp, colp), (hh, hs), (hpts, pts), (hrhs, rhs), (hy, ys))
+            ((hpiv, piv), (hpts, pts), (hcolp, colp), (hh, hs), (hrhs, rhs), (hy, ys))
         )
     ]
     for copy in copies:
         copy.start()
-    tile_rows, size, _ = pts.shape
+    tile_rows, size, feat = pts.shape
     tile_cols = colp.shape[0]
-    row_in = lax.broadcasted_iota(jnp.int32, (size, size), 0)
-    col_in = lax.broadcasted_iota(jnp.int32, (size, size), 1)
-    eye = (row_in == col_in).astype(F32)
-    lower = row_in >= col_in
-    for copy in copies:
+    high, wide = tile_rows * size, tile_cols * size
+    scale = -SCALE / feat * LOG2E
+    diagonal = lax.broadcasted_iota(jnp.int32, (size, size), 0) - lax.broadcasted_iota(
+        jnp.int32, (size, size), 1
+    )
+    eye = (diagonal == 0).astype(F32)
+    lower = diagonal >= 0
+
+    def nugget(hit):
+        return jnp.where(hit, NUGGET, 0.0) * eye
+
+    def across(x):
+        return right3(x * (-2.0 * scale)), row_squares(x) * scale
+
+    def along(x):
+        return left3(x), jnp.sum(x * x, axis=1, keepdims=True) * scale
+
+    def covariance(a, b):
+        return jnp.exp2((nt(a[0], b[0]) + a[1]) + b[1])
+
+    for copy in copies[:3]:
         copy.wait()
-    x0, x1 = piv[0], piv[1]
-    sq0, sq1 = row_squares(x0), row_squares(x1)
-    h0s, h1s, hxs = ((hs[n, 0], hs[n, 1]) for n in range(3))
-
-    def panels_of(x, tile):
-        k0 = split(squared_exp(x, x0, sq0) + jnp.where(tile == 0, NUGGET, 0.0) * eye)
-        l0 = nt3(k0, h0s)
-        l0 = jnp.where((tile != 0) | lower, l0, 0.0)
-        k1 = split(squared_exp(x, x1, sq1) + jnp.where(tile == 1, NUGGET, 0.0) * eye)
-        l1 = nt3(k0, hxs) + nt3(k1, h1s)
-        l1 = jnp.where((tile > 1) | (lower & (tile == 1)), l1, 0.0)
-        return l0, l1
-
-    for c2 in range(tile_cols):
-        l0, l1 = panels_of(colp[c2], c2 * cols_n + col_id)
-        lh[c2, :, :size], ll[c2, :, :size] = split(l0)
-        lh[c2, :, size:], ll[c2, :, size:] = split(l1)
-    yv = ys[...]
-    y = split(yv)
-
-    writes = []
+    pivots = [across(piv[k]) for k in range(PANELS)]
+    rows = along(pts[...].reshape(high, feat))
+    xc = colp[...].reshape(wide, feat)
+    cols = along(xc)
+    for k in range(PANELS):
+        for start, x, tile in ((0, rows, row_id), (high, cols, col_id)):
+            value = covariance(x, pivots[k])
+            top = left3(value[:size] + nugget(tile == k))
+            k3[start : start + size, 3 * k * size : 3 * (k + 1) * size] = top
+            k3[start + size : start + x[0].shape[0], 3 * k * size : 3 * (k + 1) * size] = left3(value[size:])
+
+    copies[3].wait()
+    for start, count, tile in ((high, wide, col_id), (0, high, row_id)):
+        l0 = nt(k3[start : start + count, : 3 * size], hs[:, : 3 * size])
+        l1 = nt(k3[start : start + count, :], hs[:, 3 * size :])
+        for k, value in ((0, l0), (1, l1)):
+            top = jnp.where((tile > k) | (lower & (tile == k)), value[:size], 0.0)
+            for at, part in ((0, top), (size, value[size:])):
+                hi, lo = split(part)
+                span = pl.ds(at, part.shape[0])
+                order = (hi, lo, hi) if start else (hi, hi, lo)
+                for n, piece in enumerate(order):
+                    place = pl.ds((PANELS * n + k) * size, size)
+                    (lc3 if start else lr3)[span, place] = piece
+
+    def put(a, c2, value):
+        for half in range(size // 128):
+            stage[a, pl.ds(c2 * (size // 128) + half, size, stride=wide // 128), :] = value[
+                :, half * 128 : half * 128 + 128
+            ]
+
+    def schur(c2, begin, end):
+        tile_c = c2 * cols_n + col_id
+        value = covariance((rows[0][begin * size : end * size], rows[1][begin * size : end * size]), across(colp[c2]))
+        value = value - nt(lr3[begin * size : end * size, :], lc3[c2 * size : (c2 + 1) * size, :])
+        for a in range(begin, end):
+            tile = a * rows_n + row_id
+            part = value[(a - begin) * size : (a - begin + 1) * size] + nugget(tile == tile_c)
+            put(a, c2, jnp.where(tile >= PANELS, part, 0.0) if a == 0 else part)
+
+    @pl.when(col_id >= PANELS)
+    def _():
+        schur(0, 0, tile_rows)
+
+    for k in range(PANELS):
+
+        @pl.when(col_id == k)
+        def _(k=k):
+            for a in range(tile_rows):
+                span = pl.ds(a * size, size)
+                hi = lr3[span, k * size : (k + 1) * size].astype(F32)
+                put(a, 0, hi + lr3[span, (2 * PANELS + k) * size : (2 * PANELS + k + 1) * size].astype(F32))
+
+    for copy in copies[4:]:
+        copy.wait()
+    width = ys.shape[0]
+    y = ys[...]
+    filled = jnp.concatenate([y, jnp.zeros((128 - width, y.shape[1]), F32)], axis=0) if width < 128 else y
+    update = nt(lr3[...], right3(filled))
     for a in range(tile_rows):
         tile = a * rows_n + row_id
-        x = pts[a]
-        l0, l1 = panels_of(x, tile)
-        ls = split(jnp.concatenate([l0, l1], axis=1))
-        left = rhs[a] - nt3(y, ls)
-        rest[a] = jnp.where(tile == 0, yv[:, :size], jnp.where(tile == 1, yv[:, size:], left))
-        for c2 in range(tile_cols):
-            tile_c = c2 * cols_n + col_id
-            xc = colp[c2]
-            k = squared_exp(x, xc, row_squares(xc)) + jnp.where(tile == tile_c, NUGGET, 0.0) * eye
-            s = k - nt3(ls, (lh[c2], ll[c2]))
-            s = jnp.where(tile >= PANELS, s, 0.0)
-            if c2 == 0:
-                s = jnp.where(tile_c == 0, l0, jnp.where(tile_c == 1, l1, s))
-            for half in range(size // 128):
-                stage[a, pl.ds(c2 * (size // 128) + half, size, stride=tile_cols * size // 128), :] = s[
-                    :, half * 128 : half * 128 + 128
-                ]
-        writes.append(pltpu.make_async_copy(stage.at[a], out.at[a], osems.at[a]))
-        writes[-1].start()
-    writes.append(pltpu.make_async_copy(rest, solved, osems.at[tile_rows]))
-    writes[-1].start()
+        turned = jnp.concatenate(
+            [update[a * size + n : a * size + n + 128].T[:width] for n in range(0, size, 128)], axis=1
+        )
+        value = rhs[a] - turned
+        if a == 0:
+            for k in range(PANELS):
+                value = jnp.where(tile == k, y[:, k * size : (k + 1) * size], value)
+        rest[a] = value
+    writes = [pltpu.make_async_copy(rest, solved, osems.at[tile_rows])]
+    writes[0].start()
+
+    for c2 in range(1, tile_cols):
+        for begin in range(0, tile_rows, 2):
+            end = min(begin + 2, tile_rows)
+            schur(c2, begin, end)
+            if c2 == tile_cols - 1:
+                for a in range(begin, end):
+                    writes.append(pltpu.make_async_copy(stage.at[a], out.at[a], osems.at[a]))
+                    writes[-1].start()
     for copy in writes:
         copy.wait()
 
@@ -367,10 +454,10 @@
     tile_cols = tile_rows * rows_n // cols_n
     pts = points[:, 0]
     right = rhs[:, 0].swapaxes(1, 2)
-    jobs = 2 * PANELS + tile_cols
+    jobs = 2 * PANELS + tile_cols + 1
     hbm = pl.BlockSpec(memory_space=pltpu.HBM)
     piv_s, colp_s = (PANELS, size, feat), (tile_cols, size, feat)
-    h_s, y_s = (3, 2, size, size), (width, PANELS * size)
+    h_s, y_s = (size, 9 * size), (width, PANELS * size)
     piv, colp, hs, ys = pl.pallas_call(
         functools.partial(factor_kernel, rows_n, cols_n, tile_cols),
         out_shape=(
@@ -416,8 +503,9 @@
             pltpu.VMEM(right.shape, F32),
             pltpu.VMEM(h_s, BF16),
             pltpu.VMEM(y_s, F32),
-            pltpu.VMEM((tile_cols, size, PANELS * size), BF16),
-            pltpu.VMEM((tile_cols, size, PANELS * size), BF16),
+            pltpu.VMEM(((tile_rows + tile_cols) * size, 3 * PANELS * size), BF16),
+            pltpu.VMEM((tile_rows * size, 3 * PANELS * size), BF16),
+            pltpu.VMEM((tile_cols * size, 3 * PANELS * size), BF16),
             pltpu.VMEM(out_s, F32),
             pltpu.VMEM((tile_rows, width, size), F32),
             pltpu.SemaphoreType.DMA((6,)),

time: 35.5 us -> 33 us (0.930)
  Pallas kernels: 34.5 us -> 32.1 us
    pallas_call x1, Pallas kernels: 12.1 us -> 10.8 us  [per_device(): pl.pallas_call(functools.partial(tiles_kernel, rows_n, cols_n), out_shape...]
    pallas_call x1, Pallas kernels: 22.4 us -> 21.3 us  [per_device(): pl.pallas_call(functools.partial(factor_kernel, rows_n, cols_n, tile_cols...]
where the time goes in v3:
time: 33 us; the launch traced here: 32.9 us
  Pallas kernels  32.1 us (97%)
  between operations  0.8 us (2%)
    pallas_call x1, Pallas kernels, per_device(): pl.pallas_call(functools.partial(factor_kernel, rows_n, cols_n, tile_cols...  21.3 us
    pallas_call x1, Pallas kernels, per_device(): pl.pallas_call(functools.partial(tiles_kernel, rows_n, cols_n), out_shape...  10.8 us

profile of v3, /device:TPU:29, one launch (start us, length us, event | category | flops | bytes accessed | tf_op | source)
XLA Modules:
  0.0 32.9 jit_solution(1555300544493810214)
XLA Ops:
  0.6 21.3 %factor.1 = (f32[2,256,128]{2,1,0:T(8,128)}, f32[2,256,128]{2,1,0:T(8,128)}, bf16[256,2304]{1,0:T(8,128)(2,1)}, f32[32,512]{1,0:T(8,128)}) custom-call(f32[4,256,128]{2,1,0:T(8,128)} %bitcast.10, f32[4,32,256]{2,1,0:T(8,128)} %bitcast.12), custom_call_target="tpu_custom_call" | custom-call | tf_op jit(solution)/shard_map/factor/pallas_call | solution.py:461
  21.9 10.8 %tiles.1 = (f32[4,1024,128]{2,1,0:T(8,128)}, f32[4,32,256]{2,1,0:T(8,128)}) custom-call(f32[4,256,128]{2,1,0:T(8,128)} %bitcast.11, f32[2,256,128]{2,1,0:T(8,128)} %get-tuple-element.8.hpiv, f32[2,256,128]{2,1,0:T(8,128)} %get-tuple-element.9.hcolp, f32[4,32,256]{2,1,0:T(8,128)} %bitcast.13, bf16[256,2304]{1,0:T(8,128)(2,1)} %get-tuple-element.10.hh, ...), custom_call_target="tpu_custom_call" | custom-call | tf_op jit(solution)/shard_map/tiles/pallas_call | solution.py:491

commit v4 on v3

--- a/solution.py
+++ b/solution.py
@@ -15,6 +15,7 @@
 F32 = jnp.float32
 BF16 = jnp.bfloat16
 NB = 128
+DIRECT = (1, 2)
 LOG2E = 1.4426950408889634
 
 
@@ -126,8 +127,8 @@
 
 
 def factor_kernel(
-    rows_n, cols_n, tile_cols, pts, prhs, opiv, ocolp, oh, oy,
-    piv, colp, rpiv, w, h0, h1, hs, ys, send, recv, local, wsem,
+    rows_n, cols_n, tile_cols, pts, prhs, opiv, ocolp, oh, orpiv,
+    piv, colp, rpiv, w, h0, h1, hs, send, recv, local, wsem,
 ):
     row_id = lax.axis_index("row")
     col_id = lax.axis_index("col")
@@ -155,7 +156,7 @@
 
     def remote(number, half, dest, slot, relay=False):
         _, src, dst = jobs[number]
-        if number == 1:
+        if number in DIRECT:
             return pltpu.make_async_remote_copy(
                 src_ref=src,
                 dst_ref=dst,
@@ -179,7 +180,7 @@
             for half in range(2):
                 dest = 2 * lax.rem(chip + step, chips) + half
                 out.append(remote(number, half, dest, 2 * step + half))
-        return out + [remote(number, half, sibling, half) for half in range(1 if number == 1 else 2)]
+        return out + [remote(number, half, sibling, half) for half in range(1 if number in DIRECT else 2)]
 
     def own(number):
         _, src, dst = jobs[number]
@@ -208,6 +209,12 @@
         def _():
             own(number).wait()
 
+        if number in DIRECT:
+            @when(row_id != owner)
+            def _():
+                remote(number, 0, sibling, 0).wait_recv()
+            return
+
         @when(sibling == owner)
         def _():
             for half in range(2):
@@ -224,6 +231,9 @@
         def _():
             for copy in sends(number):
                 copy.wait_send()
+
+        if number in DIRECT:
+            return
 
         @when(chip != owner // 2)
         def _():
@@ -239,7 +249,7 @@
     relay(0)
     arrive(0)
     drain(0)
-    for number in range(1, len(jobs)):
+    for number in DIRECT:
         launch(number)
 
     size = piv.shape[1]
@@ -250,15 +260,9 @@
     sqa = row_squares(xa)
     w[:NB, :NB] = squared_exp(xa, xa, sqa) + NUGGET * eye[:NB, :NB]
     inv = base_inverse(w[:NB, :NB])
-
-    @when(row_id == 0)
-    def _():
-        own(1).wait()
-
-    @when(row_id != 0)
-    def _():
-        remote(1, 0, 0, 0).wait_recv()
-
+    for number in range(3, len(jobs)):
+        launch(number)
+    arrive(1)
     xb = piv[0, NB:]
     w[NB:, :NB] = squared_exp(xb, xa, sqa)
     w[NB:, NB:] = squared_exp(xb, xb, row_squares(xb)) + NUGGET * eye[:NB, :NB]
@@ -266,41 +270,30 @@
     x0 = piv[0]
     sq0 = row_squares(x0)
     h0s = split(h0[...])
-    hs[:, : 3 * size] = right3(h0[...])
-
-    for number in range(2, len(jobs)):
-        relay(number)
+    hs[0, 0], hs[0, 1] = h0s
     arrive(2)
     x1 = piv[1]
     sq1 = row_squares(x1)
     l10s = split(nt3(split(squared_exp(x1, x0, sq0)), h0s))
     w[...] = squared_exp(x1, x1, sq1) + NUGGET * eye - nt3(l10s, l10s)
     mixed = split(nn3(l10s, h0s))
-    inverse_factor(w, h1, base_inverse(w[:NB, :NB]))
-
+    inv = base_inverse(w[:NB, :NB])
+    for number in range(3, len(jobs)):
+        relay(number)
+    inverse_factor(w, h1, inv)
     for number in range(3, len(jobs)):
         arrive(number)
-    writes = [pltpu.make_async_copy(piv, opiv, wsem.at[0]), pltpu.make_async_copy(colp, ocolp, wsem.at[1])]
+    writes = [
+        pltpu.make_async_copy(src, dst, wsem.at[n]) for n, (src, dst) in enumerate(((piv, opiv), (colp, ocolp), (rpiv, orpiv)))
+    ]
     for copy in writes:
         copy.start()
     h1s = split(h1[...])
-    hx = -nn3(h1s, mixed)
-    hxs = split(hx)
-    hs[:, 3 * size : 6 * size] = right3(hx)
-    hs[:, 6 * size :] = right3(h1[...])
-    writes.append(pltpu.make_async_copy(hs, oh, wsem.at[2]))
+    hs[1, 0], hs[1, 1] = h1s
+    hs[2, 0], hs[2, 1] = split(-nn3(h1s, mixed))
+    writes.append(pltpu.make_async_copy(hs, oh, wsem.at[3]))
     writes[-1].start()
-    r0, r1 = split(rpiv[0]), split(rpiv[1])
-    ys[:, :size] = nt3(r0, h0s)
-    ys[:, size:] = nt3(r0, hxs) + nt3(r1, h1s)
-    writes.append(pltpu.make_async_copy(ys, oy, wsem.at[3]))
-    writes[-1].start()
-    @when(row_id == 0)
-    def _():
-        for copy in sends(1):
-            copy.wait_send()
-
-    for number in range(2, len(jobs)):
+    for number in range(1, len(jobs)):
         drain(number)
     for copy in writes:
         copy.wait()
@@ -325,15 +318,15 @@
 
 
 def tiles_kernel(
-    rows_n, cols_n, hpts, hpiv, hcolp, hrhs, hh, hy, out, solved,
-    pts, piv, colp, rhs, hs, ys, k3, lr3, lc3, stage, rest, sems, osems,
+    rows_n, cols_n, hpts, hpiv, hcolp, hrhs, hh, hr, out, solved,
+    pts, piv, colp, rhs, hs, rpiv, k3, lc3, stage, rest, sems, osems,
 ):
     row_id = lax.axis_index("row")
     col_id = lax.axis_index("col")
     copies = [
         pltpu.make_async_copy(src, dst, sems.at[n])
         for n, (src, dst) in enumerate(
-            ((hpiv, piv), (hpts, pts), (hcolp, colp), (hh, hs), (hrhs, rhs), (hy, ys))
+            ((hpiv, piv), (hpts, pts), (hcolp, colp), (hh, hs), (hr, rpiv), (hrhs, rhs))
         )
     ]
     for copy in copies:
@@ -363,29 +356,40 @@
     for copy in copies[:3]:
         copy.wait()
     pivots = [across(piv[k]) for k in range(PANELS)]
-    rows = along(pts[...].reshape(high, feat))
     xc = colp[...].reshape(wide, feat)
-    cols = along(xc)
+
+    def spread(ref, value, k, order):
+        pieces = split(value)
+        for n, which in enumerate(order):
+            ref[:, pl.ds((PANELS * n + k) * size, size)] = pieces[which]
+
+    def pivot_tiles(x, tile):
+        side = along(x)
+        values = []
+        for k in range(PANELS):
+            value = covariance(side, pivots[k])
+            values.append(jnp.concatenate([value[:size] + nugget(tile == k), value[size:]], axis=0))
+        return values
+
+    kc = pivot_tiles(xc, col_id)
+    copies[3].wait()
+    copies[4].wait()
+    width = rpiv.shape[1]
+    padding = [jnp.zeros((-width % 16, size), F32)] if width % 16 else []
+    kc = [split(jnp.concatenate([kc[k], rpiv[k]] + padding, axis=0)) for k in range(PANELS)]
+    h0s, h1s, hxs = ((hs[n, 0], hs[n, 1]) for n in range(3))
+    l0 = nt3(kc[0], h0s)
+    l1 = nt3(kc[0], hxs) + nt3(kc[1], h1s)
+    l0s, l1s = split(l0), split(l1)
+    weighted = nn3(l0s, h0s) + nn3(l1s, hxs), nn3(l1s, h1s)
     for k in range(PANELS):
-        for start, x, tile in ((0, rows, row_id), (high, cols, col_id)):
-            value = covariance(x, pivots[k])
-            top = left3(value[:size] + nugget(tile == k))
-            k3[start : start + size, 3 * k * size : 3 * (k + 1) * size] = top
-            k3[start + size : start + x[0].shape[0], 3 * k * size : 3 * (k + 1) * size] = left3(value[size:])
-
-    copies[3].wait()
-    for start, count, tile in ((high, wide, col_id), (0, high, row_id)):
-        l0 = nt(k3[start : start + count, : 3 * size], hs[:, : 3 * size])
-        l1 = nt(k3[start : start + count, :], hs[:, 3 * size :])
-        for k, value in ((0, l0), (1, l1)):
-            top = jnp.where((tile > k) | (lower & (tile == k)), value[:size], 0.0)
-            for at, part in ((0, top), (size, value[size:])):
-                hi, lo = split(part)
-                span = pl.ds(at, part.shape[0])
-                order = (hi, lo, hi) if start else (hi, hi, lo)
-                for n, piece in enumerate(order):
-                    place = pl.ds((PANELS * n + k) * size, size)
-                    (lc3 if start else lr3)[span, place] = piece
+        spread(lc3, weighted[k][:wide], k, (0, 1, 0))
+    ys = l0[wide : wide + width], l1[wide : wide + width]
+    z = split(jnp.concatenate([value[wide : wide + width] for value in weighted], axis=1))
+    xr = pts[...].reshape(high, feat)
+    rows = along(xr)
+    for k, value in enumerate(pivot_tiles(xr, row_id)):
+        spread(k3, value, k, (0, 0, 1))
 
     def put(a, c2, value):
         for half in range(size // 128):
@@ -396,7 +400,7 @@
     def schur(c2, begin, end):
         tile_c = c2 * cols_n + col_id
         value = covariance((rows[0][begin * size : end * size], rows[1][begin * size : end * size]), across(colp[c2]))
-        value = value - nt(lr3[begin * size : end * size, :], lc3[c2 * size : (c2 + 1) * size, :])
+        value = value - nt(k3[begin * size : end * size, :], lc3[c2 * size : (c2 + 1) * size, :])
         for a in range(begin, end):
             tile = a * rows_n + row_id
             part = value[(a - begin) * size : (a - begin + 1) * size] + nugget(tile == tile_c)
@@ -406,30 +410,40 @@
     def _():
         schur(0, 0, tile_rows)
 
+    def panel(k):
+        halves = [
+            (k3[:, j * size : (j + 1) * size], k3[:, (2 * PANELS + j) * size : (2 * PANELS + j + 1) * size])
+            for j in range(PANELS)
+        ]
+        value = nt3(halves[0], h0s) if k == 0 else nt3(halves[0], hxs) + nt3(halves[1], h1s)
+        top = jnp.where((row_id > k) | (lower & (row_id == k)), value[:size], 0.0)
+        for a in range(tile_rows):
+            put(a, 0, value[a * size : (a + 1) * size] if a else top)
+
     for k in range(PANELS):
 
         @pl.when(col_id == k)
         def _(k=k):
-            for a in range(tile_rows):
-                span = pl.ds(a * size, size)
-                hi = lr3[span, k * size : (k + 1) * size].astype(F32)
-                put(a, 0, hi + lr3[span, (2 * PANELS + k) * size : (2 * PANELS + k + 1) * size].astype(F32))
-
-    for copy in copies[4:]:
-        copy.wait()
-    width = ys.shape[0]
-    y = ys[...]
-    filled = jnp.concatenate([y, jnp.zeros((128 - width, y.shape[1]), F32)], axis=0) if width < 128 else y
-    update = nt(lr3[...], right3(filled))
+            panel(k)
+
+    copies[5].wait()
+    z = [piece.astype(F32) for piece in z]
+    room = max(NB, 2 * width)
+    filled = jnp.concatenate(
+        [jnp.concatenate([piece, piece], axis=1) for piece in z]
+        + ([jnp.zeros((room - 2 * width, 2 * PANELS * size), F32)] if room > 2 * width else []),
+        axis=0,
+    ).astype(BF16)
+    update = nt(k3[:, PANELS * size :], filled)
     for a in range(tile_rows):
         tile = a * rows_n + row_id
         turned = jnp.concatenate(
-            [update[a * size + n : a * size + n + 128].T[:width] for n in range(0, size, 128)], axis=1
+            [update[a * size + n : a * size + n + 128].T for n in range(0, size, 128)], axis=1
         )
-        value = rhs[a] - turned
+        value = rhs[a] - (turned[:width] + turned[width : 2 * width])
         if a == 0:
             for k in range(PANELS):
-                value = jnp.where(tile == k, y[:, k * size : (k + 1) * size], value)
+                value = jnp.where(tile == k, ys[k], value)
         rest[a] = value
     writes = [pltpu.make_async_copy(rest, solved, osems.at[tile_rows])]
     writes[0].start()
@@ -457,26 +471,25 @@
     jobs = 2 * PANELS + tile_cols + 1
     hbm = pl.BlockSpec(memory_space=pltpu.HBM)
     piv_s, colp_s = (PANELS, size, feat), (tile_cols, size, feat)
-    h_s, y_s = (size, 9 * size), (width, PANELS * size)
-    piv, colp, hs, ys = pl.pallas_call(
+    h_s, r_s = (3, 2, size, size), (PANELS, width, size)
+    piv, colp, hs, rpiv = pl.pallas_call(
         functools.partial(factor_kernel, rows_n, cols_n, tile_cols),
         out_shape=(
             jax.ShapeDtypeStruct(piv_s, F32),
             jax.ShapeDtypeStruct(colp_s, F32),
             jax.ShapeDtypeStruct(h_s, BF16),
-            jax.ShapeDtypeStruct(y_s, F32),
+            jax.ShapeDtypeStruct(r_s, F32),
         ),
         in_specs=[hbm] * 2,
         out_specs=(hbm,) * 4,
         scratch_shapes=[
             pltpu.VMEM(piv_s, F32),
             pltpu.VMEM(colp_s, F32),
-            pltpu.VMEM((PANELS, width, size), F32),
+            pltpu.VMEM(r_s, F32),
             pltpu.VMEM((size, size), F32),
             pltpu.VMEM((size, size), F32),
             pltpu.VMEM((size, size), F32),
             pltpu.VMEM(h_s, BF16),
-            pltpu.VMEM(y_s, F32),
             pltpu.SemaphoreType.DMA((jobs, rows_n)),
             pltpu.SemaphoreType.DMA((jobs, 2)),
             pltpu.SemaphoreType.DMA((jobs,)),
@@ -502,8 +515,7 @@
             pltpu.VMEM(colp_s, F32),
             pltpu.VMEM(right.shape, F32),
             pltpu.VMEM(h_s, BF16),
-            pltpu.VMEM(y_s, F32),
-            pltpu.VMEM(((tile_rows + tile_cols) * size, 3 * PANELS * size), BF16),
+            pltpu.VMEM(r_s, F32),
             pltpu.VMEM((tile_rows * size, 3 * PANELS * size), BF16),
             pltpu.VMEM((tile_cols * size, 3 * PANELS * size), BF16),
             pltpu.VMEM(out_s, F32),
@@ -513,7 +525,7 @@
         ],
         compiler_params=pltpu.CompilerParams(vmem_limit_bytes=62 * 1024 * 1024),
         name="tiles",
-    )(pts, piv, colp, right, hs, ys)
+    )(pts, piv, colp, right, hs, rpiv)
     factored = factored.reshape(tile_rows, 1, size, tile_cols, 1, size)
     return factored, solved.swapaxes(1, 2)[:, None]
 

time: 33 us -> 30.5 us (0.924)
  Pallas kernels: 32.1 us -> 29.6 us
    pallas_call x1, Pallas kernels: 10.8 us -> 9.12 us  [per_device(): pl.pallas_call(functools.partial(tiles_kernel, rows_n, cols_n), out_shape...]
    pallas_call x1, Pallas kernels: 21.3 us -> 20.4 us  [per_device(): pl.pallas_call(functools.partial(factor_kernel, rows_n, cols_n, tile_cols...]
where the time goes in v4:
time: 30.5 us; the launch traced here: 30.3 us
  Pallas kernels  29.6 us (97%)
  between operations  0.8 us (3%)
    pallas_call x1, Pallas kernels, per_device(): pl.pallas_call(functools.partial(factor_kernel, rows_n, cols_n, tile_cols...  20.4 us
    pallas_call x1, Pallas kernels, per_device(): pl.pallas_call(functools.partial(tiles_kernel, rows_n, cols_n), out_shape...  9.12 us

profile of v4, /device:TPU:29, one launch (start us, length us, event | category | flops | bytes accessed | tf_op | source)
XLA Modules:
  0.0 30.3 jit_solution(3654636986873975339)
XLA Ops:
  0.6 20.4 %factor.1 = (f32[2,256,128]{2,1,0:T(8,128)}, f32[2,256,128]{2,1,0:T(8,128)}, bf16[3,2,256,256]{3,2,1,0:T(8,128)(2,1)}, f32[2,32,256]{2,1,0:T(8,128)}) custom-call(f32[4,256,128]{2,1,0:T(8,128)} %bitcast.10, f32[4,32,256]{2,1,0:T(8,128)} %bitcast.12), custom_call_target="tpu_custom_call" | custom-call | tf_op jit(solution)/shard_map/factor/pallas_call | solution.py:475
  21.1 9.1 %tiles.1 = (f32[4,1024,128]{2,1,0:T(8,128)}, f32[4,32,256]{2,1,0:T(8,128)}) custom-call(f32[4,256,128]{2,1,0:T(8,128)} %bitcast.11, f32[2,256,128]{2,1,0:T(8,128)} %get-tuple-element.8.hpiv, f32[2,256,128]{2,1,0:T(8,128)} %get-tuple-element.9.hcolp, f32[4,32,256]{2,1,0:T(8,128)} %bitcast.13, bf16[3,2,256,256]{3,2,1,0:T(8,128)(2,1)} %get-tuple-element.10.hh, ...), custom_call_target="tpu_custom_call" | custom-call | tf_op jit(solution)/shard_map/tiles/pallas_call | solution.py:504

commit v5 on v4

--- a/solution.py
+++ b/solution.py
@@ -50,7 +50,7 @@
 def rowof(tile, s):
     return jnp.broadcast_to(tile[s:s+1], tile.shape)
 
-def base_inverse(block, width=16, ahead=2):
+def base_inverse(block, fill=None, width=16, ahead=2):
     lane = lax.broadcasted_iota(jnp.int32, (8, NB), 1)
     sub = lax.broadcasted_iota(jnp.int32, (8, NB), 0)
     v = [block[8 * q : 8 * q + 8] for q in range(NB // 8)]
@@ -65,6 +65,8 @@
         d[0] = [jnp.where(lane >= 0, x, 0.0) for x in d[0]]
         low = [[splat(v[q], j+n) for n in range(width)] for q in near]
         inside = (lane >= j) & (lane < j+width)
+        if fill is not None:
+            fill(j // width)
         r = [jnp.where(inside, (lane - j == sub + 8*t).astype(F32), v[q0+t]) for t in range(per)]
         f = [None]*per
         S = [None]*width
@@ -114,21 +116,21 @@
     return jnp.concatenate(out, axis=0)
 
 
-def inverse_factor(w, h, inv):
+def inverse_factor(w, h, inv, fill=None):
     h[:NB, :NB] = inv
     h[:NB, NB:] = jnp.zeros((NB, w.shape[1] - NB), F32)
     first = split(inv)
     below = split(nt3(split(w[NB:, :NB]), first))
     w[NB:, NB:] = w[NB:, NB:] - nt3(below, below)
     mixed = split(nn3(below, first))
-    inv = base_inverse(w[NB:, NB:])
+    inv = base_inverse(w[NB:, NB:], fill)
     h[NB:, NB:] = inv
     h[NB:, :NB] = -nn3(split(inv), mixed)
 
 
 def factor_kernel(
-    rows_n, cols_n, tile_cols, pts, prhs, opiv, ocolp, oh, orpiv,
-    piv, colp, rpiv, w, h0, h1, hs, send, recv, local, wsem,
+    rows_n, cols_n, tile_cols, pts, prhs, opiv, ocolp, oh, orpiv, ok2, ol3, osq,
+    piv, colp, rpiv, w, h0, h1, hs, own_pts, k2, l3, sq, send, recv, local, wsem,
 ):
     row_id = lax.axis_index("row")
     col_id = lax.axis_index("col")
@@ -244,8 +246,17 @@
         def _(number=number):
             own(number).start()
 
+    rows_copy = pltpu.make_async_copy(pts, own_pts, wsem.at[5])
+    rows_copy.start()
     pl.semaphore_wait(barrier, rows_n - 1)
     launch(0)
+    rows_copy.wait()
+    side = along(own_pts[...].reshape(l3.shape[0], own_pts.shape[2]))
+    l3[...] = side[0]
+    sq[...] = jnp.broadcast_to(side[1], sq.shape)
+    early = [pltpu.make_async_copy(l3, ol3, wsem.at[6]), pltpu.make_async_copy(sq, osq, wsem.at[7])]
+    for copy in early:
+        copy.start()
     relay(0)
     arrive(0)
     drain(0)
@@ -256,6 +267,22 @@
     eye = (
         lax.broadcasted_iota(jnp.int32, (size, size), 0) == lax.broadcasted_iota(jnp.int32, (size, size), 1)
     ).astype(F32)
+
+    def row_tiles(k):
+        b = across(piv[k])
+        step = own_pts.shape[0] * size * 16 // NB
+
+        def piece(n):
+            span = pl.ds(n * step, step)
+            value = covariance((l3[span, :], widen(sq[span, :], size)), b)
+            if n * step < size:
+                value = value + jnp.where(row_id == k, NUGGET, 0.0) * eye[n * step : (n + 1) * step]
+            hi, lo = split(value)
+            k2[span, pl.ds(k * size, size)] = hi
+            k2[span, pl.ds((PANELS + k) * size, size)] = lo
+
+        return piece
+
     xa = piv[0, :NB]
     sqa = row_squares(xa)
     w[:NB, :NB] = squared_exp(xa, xa, sqa) + NUGGET * eye[:NB, :NB]
@@ -266,9 +293,9 @@
     xb = piv[0, NB:]
     w[NB:, :NB] = squared_exp(xb, xa, sqa)
     w[NB:, NB:] = squared_exp(xb, xb, row_squares(xb)) + NUGGET * eye[:NB, :NB]
-    inverse_factor(w, h0, inv)
     x0 = piv[0]
     sq0 = row_squares(x0)
+    inverse_factor(w, h0, inv, row_tiles(0))
     h0s = split(h0[...])
     hs[0, 0], hs[0, 1] = h0s
     arrive(2)
@@ -277,16 +304,18 @@
     l10s = split(nt3(split(squared_exp(x1, x0, sq0)), h0s))
     w[...] = squared_exp(x1, x1, sq1) + NUGGET * eye - nt3(l10s, l10s)
     mixed = split(nn3(l10s, h0s))
-    inv = base_inverse(w[:NB, :NB])
+    inv = base_inverse(w[:NB, :NB], row_tiles(1))
+    writes = [pltpu.make_async_copy(k2, ok2, wsem.at[4])]
+    writes[0].start()
     for number in range(3, len(jobs)):
         relay(number)
     inverse_factor(w, h1, inv)
     for number in range(3, len(jobs)):
         arrive(number)
-    writes = [
+    writes += early + [
         pltpu.make_async_copy(src, dst, wsem.at[n]) for n, (src, dst) in enumerate(((piv, opiv), (colp, ocolp), (rpiv, orpiv)))
     ]
-    for copy in writes:
+    for copy in writes[3:]:
         copy.start()
     h1s = split(h1[...])
     hs[1, 0], hs[1, 1] = h1s
@@ -307,6 +336,27 @@
     return nn(a[0], b[0]) + (nn(a[0], b[1]) + nn(a[1], b[0]))
 
 
+def scale_of(feat):
+    return -SCALE / feat * LOG2E
+
+
+def across(x):
+    scale = scale_of(x.shape[1])
+    return right3(x * (-2.0 * scale)), row_squares(x) * scale
+
+
+def along(x):
+    return left3(x), jnp.sum(x * x, axis=1, keepdims=True) * scale_of(x.shape[1])
+
+
+def covariance(a, b):
+    return jnp.exp2((nt(a[0], b[0]) + a[1]) + b[1])
+
+
+def widen(x, size):
+    return jnp.concatenate([x] * (size // x.shape[1]), axis=1)
+
+
 def left3(x):
     hi, lo = split(x)
     return jnp.concatenate([hi, hi, lo], axis=1)
@@ -318,23 +368,22 @@
 
 
 def tiles_kernel(
-    rows_n, cols_n, hpts, hpiv, hcolp, hrhs, hh, hr, out, solved,
-    pts, piv, colp, rhs, hs, rpiv, k3, lc3, stage, rest, sems, osems,
+    rows_n, cols_n, hpts, hpiv, hcolp, hrhs, hh, hr, hk2, hsq, out, solved,
+    pts, sq, piv, colp, rhs, hs, rpiv, k2, lc3, stage, rest, sems, osems,
 ):
     row_id = lax.axis_index("row")
     col_id = lax.axis_index("col")
     copies = [
         pltpu.make_async_copy(src, dst, sems.at[n])
         for n, (src, dst) in enumerate(
-            ((hpiv, piv), (hpts, pts), (hcolp, colp), (hh, hs), (hr, rpiv), (hrhs, rhs))
+            ((hpiv, piv), (hcolp, colp), (hpts, pts), (hh, hs), (hr, rpiv), (hk2, k2), (hrhs, rhs), (hsq, sq))
         )
     ]
     for copy in copies:
         copy.start()
-    tile_rows, size, feat = pts.shape
-    tile_cols = colp.shape[0]
+    tile_cols, size, feat = colp.shape
+    tile_rows = pts.shape[0] // size
     high, wide = tile_rows * size, tile_cols * size
-    scale = -SCALE / feat * LOG2E
     diagonal = lax.broadcasted_iota(jnp.int32, (size, size), 0) - lax.broadcasted_iota(
         jnp.int32, (size, size), 1
     )
@@ -344,16 +393,7 @@
     def nugget(hit):
         return jnp.where(hit, NUGGET, 0.0) * eye
 
-    def across(x):
-        return right3(x * (-2.0 * scale)), row_squares(x) * scale
-
-    def along(x):
-        return left3(x), jnp.sum(x * x, axis=1, keepdims=True) * scale
-
-    def covariance(a, b):
-        return jnp.exp2((nt(a[0], b[0]) + a[1]) + b[1])
-
-    for copy in copies[:3]:
+    for copy in copies[:2]:
         copy.wait()
     pivots = [across(piv[k]) for k in range(PANELS)]
     xc = colp[...].reshape(wide, feat)
@@ -386,10 +426,13 @@
         spread(lc3, weighted[k][:wide], k, (0, 1, 0))
     ys = l0[wide : wide + width], l1[wide : wide + width]
     z = split(jnp.concatenate([value[wide : wide + width] for value in weighted], axis=1))
-    xr = pts[...].reshape(high, feat)
-    rows = along(xr)
-    for k, value in enumerate(pivot_tiles(xr, row_id)):
-        spread(k3, value, k, (0, 0, 1))
+    copies[2].wait()
+    copies[7].wait()
+    copies[5].wait()
+
+    def stacked(begin, end):
+        span = pl.ds(begin * size, (end - begin) * size)
+        return jnp.concatenate([k2[span, : PANELS * size], k2[span, :]], axis=1)
 
     def put(a, c2, value):
         for half in range(size // 128):
@@ -399,8 +442,8 @@
 
     def schur(c2, begin, end):
         tile_c = c2 * cols_n + col_id
-        value = covariance((rows[0][begin * size : end * size], rows[1][begin * size : end * size]), across(colp[c2]))
-        value = value - nt(k3[begin * size : end * size, :], lc3[c2 * size : (c2 + 1) * size, :])
+        value = covariance((pts[begin * size : end * size, :], widen(sq[begin * size : end * size, :], size)), across(colp[c2]))
+        value = value - nt(stacked(begin, end), lc3[c2 * size : (c2 + 1) * size, :])
         for a in range(begin, end):
             tile = a * rows_n + row_id
             part = value[(a - begin) * size : (a - begin + 1) * size] + nugget(tile == tile_c)
@@ -412,7 +455,7 @@
 
     def panel(k):
         halves = [
-            (k3[:, j * size : (j + 1) * size], k3[:, (2 * PANELS + j) * size : (2 * PANELS + j + 1) * size])
+            (k2[:, j * size : (j + 1) * size], k2[:, (PANELS + j) * size : (PANELS + j + 1) * size])
             for j in range(PANELS)
         ]
         value = nt3(halves[0], h0s) if k == 0 else nt3(halves[0], hxs) + nt3(halves[1], h1s)
@@ -426,7 +469,7 @@
         def _(k=k):
             panel(k)
 
-    copies[5].wait()
+    copies[6].wait()
     z = [piece.astype(F32) for piece in z]
     room = max(NB, 2 * width)
     filled = jnp.concatenate(
@@ -434,7 +477,7 @@
         + ([jnp.zeros((room - 2 * width, 2 * PANELS * size), F32)] if room > 2 * width else []),
         axis=0,
     ).astype(BF16)
-    update = nt(k3[:, PANELS * size :], filled)
+    update = nt(k2[...], filled)
     for a in range(tile_rows):
         tile = a * rows_n + row_id
         turned = jnp.concatenate(
@@ -472,16 +515,21 @@
     hbm = pl.BlockSpec(memory_space=pltpu.HBM)
     piv_s, colp_s = (PANELS, size, feat), (tile_cols, size, feat)
     h_s, r_s = (3, 2, size, size), (PANELS, width, size)
-    piv, colp, hs, rpiv = pl.pallas_call(
+    k_s = (tile_rows * size, 2 * PANELS * size)
+    l_s, q_s = (tile_rows * size, 3 * feat), (tile_rows * size, 128)
+    piv, colp, hs, rpiv, k2, l3, sq = pl.pallas_call(
         functools.partial(factor_kernel, rows_n, cols_n, tile_cols),
         out_shape=(
             jax.ShapeDtypeStruct(piv_s, F32),
             jax.ShapeDtypeStruct(colp_s, F32),
             jax.ShapeDtypeStruct(h_s, BF16),
             jax.ShapeDtypeStruct(r_s, F32),
+            jax.ShapeDtypeStruct(k_s, BF16),
+            jax.ShapeDtypeStruct(l_s, BF16),
+            jax.ShapeDtypeStruct(q_s, F32),
         ),
         in_specs=[hbm] * 2,
-        out_specs=(hbm,) * 4,
+        out_specs=(hbm,) * 7,
         scratch_shapes=[
             pltpu.VMEM(piv_s, F32),
             pltpu.VMEM(colp_s, F32),
@@ -490,10 +538,14 @@
             pltpu.VMEM((size, size), F32),
             pltpu.VMEM((size, size), F32),
             pltpu.VMEM(h_s, BF16),
+            pltpu.VMEM(pts.shape, F32),
+            pltpu.VMEM(k_s, BF16),
+            pltpu.VMEM(l_s, BF16),
+            pltpu.VMEM(q_s, F32),
             pltpu.SemaphoreType.DMA((jobs, rows_n)),
             pltpu.SemaphoreType.DMA((jobs, 2)),
             pltpu.SemaphoreType.DMA((jobs,)),
-            pltpu.SemaphoreType.DMA((4,)),
+            pltpu.SemaphoreType.DMA((8,)),
         ],
         compiler_params=pltpu.CompilerParams(
             collective_id=0, has_side_effects=True, vmem_limit_bytes=62 * 1024 * 1024
@@ -507,25 +559,26 @@
             jax.ShapeDtypeStruct(out_s, F32),
             jax.ShapeDtypeStruct((tile_rows, width, size), F32),
         ),
-        in_specs=[hbm] * 6,
+        in_specs=[hbm] * 8,
         out_specs=(hbm,) * 2,
         scratch_shapes=[
-            pltpu.VMEM(pts.shape, F32),
+            pltpu.VMEM(l_s, BF16),
+            pltpu.VMEM(q_s, F32),
             pltpu.VMEM(piv_s, F32),
             pltpu.VMEM(colp_s, F32),
             pltpu.VMEM(right.shape, F32),
             pltpu.VMEM(h_s, BF16),
             pltpu.VMEM(r_s, F32),
-            pltpu.VMEM((tile_rows * size, 3 * PANELS * size), BF16),
+            pltpu.VMEM(k_s, BF16),
             pltpu.VMEM((tile_cols * size, 3 * PANELS * size), BF16),
             pltpu.VMEM(out_s, F32),
             pltpu.VMEM((tile_rows, width, size), F32),
-            pltpu.SemaphoreType.DMA((6,)),
+            pltpu.SemaphoreType.DMA((8,)),
             pltpu.SemaphoreType.DMA((tile_rows + 1,)),
         ],
         compiler_params=pltpu.CompilerParams(vmem_limit_bytes=62 * 1024 * 1024),
         name="tiles",
-    )(pts, piv, colp, right, hs, rpiv)
+    )(l3, piv, colp, right, hs, rpiv, k2, sq)
     factored = factored.reshape(tile_rows, 1, size, tile_cols, 1, size)
     return factored, solved.swapaxes(1, 2)[:, None]
 

time: 30.5 us -> 29.8 us (0.977)
  Pallas kernels: 29.6 us -> 28.8 us
    pallas_call x1, Pallas kernels: 9.12 us -> 8.11 us  [per_device(): pl.pallas_call(functools.partial(tiles_kernel, rows_n, cols_n), out_shape...]
where the time goes in v5:
time: 29.8 us; the launch traced here: 29.6 us
  Pallas kernels  28.8 us (97%)
  between operations  0.8 us (3%)
    pallas_call x1, Pallas kernels, per_device(): pl.pallas_call(functools.partial(factor_kernel, rows_n, cols_n, tile_cols...  20.7 us
    pallas_call x1, Pallas kernels, per_device(): pl.pallas_call(functools.partial(tiles_kernel, rows_n, cols_n), out_shape...  8.11 us

profile of v5, /device:TPU:29, one launch (start us, length us, event | category | flops | bytes accessed | tf_op | source)
XLA Modules:
  0.0 29.6 jit_solution(5120978439104200513)
XLA Ops:
  0.6 20.7 %factor.1 = (f32[2,256,128]{2,1,0:T(8,128)}, f32[2,256,128]{2,1,0:T(8,128)}, bf16[3,2,256,256]{3,2,1,0:T(8,128)(2,1)}, f32[2,32,256]{2,1,0:T(8,128)}, bf16[1024,...) custom-call(f32[4,256,128]{2,1,0:T(8,128)} %bitcast.12, f32[4,32,256]{2,1,0:T(8,128)} %bitcast.10), custom_call_target="tpu_custom_call" | custom-call | tf_op jit(solution)/shard_map/factor/pallas_call | solution.py:520
  21.3 8.1 %tiles.1 = (f32[4,1024,128]{2,1,0:T(8,128)}, f32[4,32,256]{2,1,0:T(8,128)}) custom-call(bf16[1024,384]{1,0:T(8,128)(2,1)} %get-tuple-element.11.hpts, f32[2,256,128]{2,1,0:T(8,128)} %get-tuple-element.12.hpiv, f32[2,256,128]{2,1,0:T(8,128)} %get-tuple-element.13.hcolp, f32[4,32,256]{2,1,0:T(8,128)} %bitcast.11, ...), custom_call_target="tpu_custom_call" | custom-call | tf_op jit(solution)/shard_map/tiles/pallas_call | solution.py:556

commit v6 on v5

--- a/solution.py
+++ b/solution.py
@@ -179,7 +179,7 @@
     def sends(number):
         out = []
         for step in range(1, chips):
-            for half in range(2):
+            for half in (1, 0):
                 dest = 2 * lax.rem(chip + step, chips) + half
                 out.append(remote(number, half, dest, 2 * step + half))
         return out + [remote(number, half, sibling, half) for half in range(1 if number in DIRECT else 2)]

time: 29.8 us -> 29.5 us (0.990)
  Pallas kernels: 28.8 us -> 28.5 us
where the time goes in v6:
time: 29.5 us; the launch traced here: 29.3 us
  Pallas kernels  28.5 us (97%)
  between operations  0.8 us (3%)
    pallas_call x1, Pallas kernels, per_device(): pl.pallas_call(functools.partial(factor_kernel, rows_n, cols_n, tile_cols...  20.4 us
    pallas_call x1, Pallas kernels, per_device(): pl.pallas_call(functools.partial(tiles_kernel, rows_n, cols_n), out_shape...  8.11 us

profile of v6, /device:TPU:29, one launch (start us, length us, event | category | flops | bytes accessed | tf_op | source)
XLA Modules:
  0.0 29.3 jit_solution(15877718318628079384)
XLA Ops:
  0.6 20.4 %factor.1 = (f32[2,256,128]{2,1,0:T(8,128)}, f32[2,256,128]{2,1,0:T(8,128)}, bf16[3,2,256,256]{3,2,1,0:T(8,128)(2,1)}, f32[2,32,256]{2,1,0:T(8,128)}, bf16[1024,...) custom-call(f32[4,256,128]{2,1,0:T(8,128)} %bitcast.12, f32[4,32,256]{2,1,0:T(8,128)} %bitcast.10), custom_call_target="tpu_custom_call" | custom-call | tf_op jit(solution)/shard_map/factor/pallas_call | solution.py:520
  21.0 8.1 %tiles.1 = (f32[4,1024,128]{2,1,0:T(8,128)}, f32[4,32,256]{2,1,0:T(8,128)}) custom-call(bf16[1024,384]{1,0:T(8,128)(2,1)} %get-tuple-element.11.hpts, f32[2,256,128]{2,1,0:T(8,128)} %get-tuple-element.12.hpiv, f32[2,256,128]{2,1,0:T(8,128)} %get-tuple-element.13.hcolp, f32[4,32,256]{2,1,0:T(8,128)} %bitcast.11, ...), custom_call_target="tpu_custom_call" | custom-call | tf_op jit(solution)/shard_map/tiles/pallas_call | solution.py:556

commit v7 on v6

--- a/solution.py
+++ b/solution.py
@@ -33,9 +33,9 @@
 
 
 def squared_exp(a, b, b_sq):
-    a_sq = jnp.sum(a * a, axis=1, keepdims=True)
-    inner = nt3(split(a), split(b))
-    return jnp.exp((-SCALE / a.shape[1]) * (a_sq + b_sq - 2.0 * inner))
+    scale = scale_of(a.shape[1])
+    side = along(a)
+    return jnp.exp2((nt(side[0], right3(b * (-2.0 * scale))) + side[1]) + b_sq * scale)
 
 
 def row_squares(b):
@@ -260,8 +260,7 @@
     relay(0)
     arrive(0)
     drain(0)
-    for number in DIRECT:
-        launch(number)
+    launch(1)
 
     size = piv.shape[1]
     eye = (
@@ -287,6 +286,7 @@
     sqa = row_squares(xa)
     w[:NB, :NB] = squared_exp(xa, xa, sqa) + NUGGET * eye[:NB, :NB]
     inv = base_inverse(w[:NB, :NB])
+    launch(2)
     for number in range(3, len(jobs)):
         launch(number)
     arrive(1)

time: 29.5 us -> 29.6 us (level)
  no operation moved by 1% of the time
where the time goes in v7:
time: 29.6 us; the launch traced here: 29.4 us
  Pallas kernels  28.6 us (97%)
  between operations  0.8 us (3%)
    pallas_call x1, Pallas kernels, per_device(): pl.pallas_call(functools.partial(factor_kernel, rows_n, cols_n, tile_cols...  20.5 us
    pallas_call x1, Pallas kernels, per_device(): pl.pallas_call(functools.partial(tiles_kernel, rows_n, cols_n), out_shape...  8.13 us

profile of v7, /device:TPU:29, one launch (start us, length us, event | category | flops | bytes accessed | tf_op | source)
XLA Modules:
  0.0 29.4 jit_solution(11447365286404314323)
XLA Ops:
  0.6 20.5 %factor.1 = (f32[2,256,128]{2,1,0:T(8,128)}, f32[2,256,128]{2,1,0:T(8,128)}, bf16[3,2,256,256]{3,2,1,0:T(8,128)(2,1)}, f32[2,32,256]{2,1,0:T(8,128)}, bf16[1024,...) custom-call(f32[4,256,128]{2,1,0:T(8,128)} %bitcast.12, f32[4,32,256]{2,1,0:T(8,128)} %bitcast.10), custom_call_target="tpu_custom_call" | custom-call | tf_op jit(solution)/shard_map/factor/pallas_call | solution.py:520
  21.1 8.1 %tiles.1 = (f32[4,1024,128]{2,1,0:T(8,128)}, f32[4,32,256]{2,1,0:T(8,128)}) custom-call(bf16[1024,384]{1,0:T(8,128)(2,1)} %get-tuple-element.11.hpts, f32[2,256,128]{2,1,0:T(8,128)} %get-tuple-element.12.hpiv, f32[2,256,128]{2,1,0:T(8,128)} %get-tuple-element.13.hcolp, f32[4,32,256]{2,1,0:T(8,128)} %bitcast.11, ...), custom_call_target="tpu_custom_call" | custom-call | tf_op jit(solution)/shard_map/tiles/pallas_call | solution.py:556
